TPU v7x, 256 devices: a whole 4x4x8 slice. The times are simulated.
256 devices in a mesh: frame: 16 (over x, z_lo, core), row: 16 (over y, z_hi).
Axes of the slice: x: 4, y: 4, z: 8 (z_hi: 4, z_lo: 2; z = z_hi * 2 + z_lo), core: 2. Of those that a mesh axis runs over, the one named last changes fastest.
Arguments:
- query: bfloat16 [16, 32, 80, 1536], P('frame', 'row'), may hold values from -6 to 6
- key: bfloat16 [16, 32, 80, 1536], P('frame', 'row'), may hold values from -6 to 6
- value: bfloat16 [16, 32, 80, 1536], P('frame', 'row'), may hold values from -6 to 6
- key_frames: int32 [16, 4], replicated, may hold values from 0 to 15, as said below
- reach: int32 [16, 4], replicated, may hold values from 0 to 1
- used: int32 [16], replicated, may hold values from 1 to 4
Outputs:
- attended: bfloat16 [16, 32, 80, 1536], P('frame', 'row')
Inputs may be any that keep to these rules, and one draw needn't show every extreme that they name: `key_frames`: entry 0 of row f is f itself; every entry j >= 1 of row f is (f + s * 2**p) modulo 16 with s = 1 or s = -1 and 0 <= p <= 2; entries may repeat.
All inputs are finite; a program needn't handle non-finite values.
Results may differ from a plain program's by a relative error of at most 0.0055.
Values may be sent and summed in bfloat16 or wider, within the bound.
A program may use at most 256 MiB of HBM per device.

v0:
```python
import jax
import jax.numpy as jnp
from jax import lax
from jax.sharding import PartitionSpec as P

HEAD_DIM = 128


def with_halo(shard, sides, width):
    for axis, dim in sides:
        devices, length = (lax.axis_size(axis), shard.shape[dim])
        up = [(i, (i + 1) % devices) for i in range(devices - 1)]
        down = [(j, i) for i, j in up]
        last = lax.slice_in_dim(shard, length - width, length, axis=dim)
        initial = lax.slice_in_dim(shard, 0, width, axis=dim)
        before = lax.ppermute(last, axis, up)
        after = lax.ppermute(initial, axis, down)
        shard = jnp.concatenate([before, shard, after], axis=dim)
    return shard


def shifted(block, axis, distance):
    devices = range(lax.axis_size(axis))
    route = [((i - distance) % len(devices), i) for i in devices]
    return lax.ppermute(block, axis, route)


def local(query, key, value, key_frames, reach, used):
    frame_dev, rows_dev, columns, features = query.shape
    head_count = features // HEAD_DIM
    slot_count = key_frames.shape[1]
    rows_all = rows_dev * lax.axis_size("row")
    frame_here = lax.axis_index("frame")
    row_here = lax.axis_index("row")
    queries_n = frame_dev * rows_dev * columns
    score_scale = HEAD_DIM ** (-0.5)
    q_heads = query.reshape(queries_n, head_count, HEAD_DIM)
    frame_ids = frame_here * frame_dev + jnp.arange(frame_dev, dtype=jnp.int32)
    own_frames = jnp.take(key_frames, frame_ids, axis=0)
    own_reach = jnp.take(reach, frame_ids, axis=0)
    own_used = jnp.take(used, frame_ids, axis=0)
    in_use = jnp.arange(slot_count, dtype=jnp.int32)[None, :] < own_used[:, None]
    row_query = row_here * rows_dev + jnp.arange(rows_dev, dtype=jnp.int32)
    row_key = row_here * rows_dev - 1 + jnp.arange(rows_dev + 2, dtype=jnp.int32)
    inside = (row_key >= 0) & (row_key < rows_all)
    distance = jnp.abs(row_query[:, None] - row_key[None, :])
    stacked = jnp.stack([key, value])
    extended = with_halo(stacked, (("row", 2),), 1)

    def attend(carried, visiting, first_frame):
        frame_count = visiting.shape[1]
        keys_n = frame_count * (rows_dev + 2) * columns
        frames_key = first_frame + jnp.arange(frame_count, dtype=jnp.int32)
        matched = in_use[:, None, :] & (own_frames[:, None, :] == frames_key[None, :, None])
        linked = jnp.any(matched, axis=2)
        spread = jnp.max(jnp.where(matched, own_reach[:, None, :], -1), axis=2)
        allowed = (
            linked[:, :, None, None]
            & (distance[None, None] <= spread[:, :, None, None])
            & inside[None, None, None, :]
        )
        allowed = jnp.transpose(allowed, (0, 2, 1, 3))
        allowed = jnp.broadcast_to(
            allowed[:, :, None, :, :, None],
            (frame_dev, rows_dev, columns, frame_count, rows_dev + 2, columns),
        )
        allowed = allowed.reshape(queries_n, keys_n)
        old_peak, totals, weighted = carried
        k_heads = visiting[0].reshape(keys_n, head_count, HEAD_DIM)
        v_heads = visiting[1].reshape(keys_n, head_count, HEAD_DIM)
        scores = (
            jnp.einsum("qhd,khd->hqk", q_heads, k_heads, preferred_element_type=jnp.float32)
            * score_scale
        )
        scores = jnp.where(allowed[None], scores, -1e30)
        new_peak = jnp.maximum(old_peak, jnp.max(scores, axis=2))
        weights = jnp.where(allowed[None], jnp.exp(scores - new_peak[:, :, None]), 0.0)
        factor = jnp.exp(old_peak - new_peak)
        totals = totals * factor + jnp.sum(weights, axis=2)
        weights_low = weights.astype(jnp.bfloat16)
        weighted = weighted * jnp.transpose(factor)[:, :, None] + jnp.einsum(
            "hqk,khd->qhd", weights_low, v_heads, preferred_element_type=jnp.float32
        )
        return (new_peak, totals, weighted)

    initial = (
        jnp.full((head_count, queries_n), -1e30, jnp.float32),
        jnp.zeros((head_count, queries_n), jnp.float32),
        jnp.zeros((queries_n, head_count, HEAD_DIM), jnp.float32),
    )
    started = attend(initial, extended, frame_here * frame_dev)

    def advance(turn_index, loop_state):
        visiting, carried = loop_state
        visiting = shifted(visiting, "frame", 1)
        anchor = (frame_here - turn_index) % lax.axis_size("frame")
        return (visiting, attend(carried, visiting, anchor * frame_dev))

    final_block, finished = lax.fori_loop(1, lax.axis_size("frame"), advance, (extended, started))
    final_peak, totals, weighted = finished
    output = weighted / jnp.transpose(totals)[:, :, None]
    return output.reshape(query.shape).astype(jnp.bfloat16)


def solution(mesh):
    return jax.shard_map(
        local,
        mesh=mesh,
        in_specs=(
            P("frame", "row", None, None),
            P("frame", "row", None, None),
            P("frame", "row", None, None),
            P(),
            P(),
            P(),
        ),
        out_specs=P("frame", "row", None, None),
        check_vma=False,
    )
```

profile of v0, /device:TPU:80, one launch (start us, length us, event | category | flops | bytes accessed | tf_op | source)
XLA Modules:
  0.0 649.2 jit_solution(12354279956884143929)
XLA Ops:
  0.0 2.2 fusion.49
  2.3 6.4 collective-permute-start.1
  18.7 11.1 %collective-permute-done.1 = bf16[2,1,1,80,1536]{4,3,2,1,0:T(8,128)(2,1)S(1)} collective-permute-done((bf16[2,1,1,80,1536]{4,3,2,1,0:T(8,128)(2,1)}, bf16[2,1,1,80,1536]{4,3,2,1,0:T(8,128)(2,1)S(1)}, u32[]{:S(2)}, u32[]{:S(2)}) %collective-permute-start.1) | collective-permute-done | bytes 491552 | tf_op jit(solution)/shard_map/ppermute | solution.py:16
  29.8 5.9 collective-permute-done.2
  44.0 4.1 fusion.43
  48.1 598.2 %while.24 = (s32[]{:T(128)}, bf16[2,1,4,80,1536]{4,3,2,1,0:T(8,128)(2,1)}, f32[12,160]{1,0:T(8,128)S(1)}, f32[12,160]{1,0:T(8,128)S(1)}, f32[160,12,128]{2,0,1:T...) while((s32[]{:T(128)}, ...), condition=%wide.region_9.11_spmd.clone, body=%wide.region_4.0_spmd.clone.sunk | while | flops 323057376 | bytes 43684368 | solution.py:99
  51.2 23.3 %collective-permute-done = bf16[2,1,4,80,1536]{4,3,2,1,0:T(8,128)(2,1)S(1)} collective-permute-done((bf16[2,1,4,80,1536]{4,3,2,1,0:T(8,128)(2,1)}, bf16[2,1,4,80,1536]{4,3,2,1,0:T(8,128)(2,1)S(1)}, u32[]{:S(2)}, u32[]{:S(2)}) %collective-permute-start) | collective-permute-done | bytes 1966112 | tf_op jit(solution)/shard_map/while/body/eval_jaxpr/ppermute | solution.py:25
  76.0 2.2 squeeze.24
  78.2 2.9 squeeze.25
  81.1 2.2 fusion.74
  91.1 23.3 %collective-permute-done = bf16[2,1,4,80,1536]{4,3,2,1,0:T(8,128)(2,1)S(1)} collective-permute-done((bf16[2,1,4,80,1536]{4,3,2,1,0:T(8,128)(2,1)}, bf16[2,1,4,80,1536]{4,3,2,1,0:T(8,128)(2,1)S(1)}, u32[]{:S(2)}, u32[]{:S(2)}) %collective-permute-start) | collective-permute-done | bytes 1966112 | tf_op jit(solution)/shard_map/while/body/eval_jaxpr/ppermute | solution.py:25
  115.8 2.2 squeeze.24
  118.1 2.9 squeeze.25
  121.0 2.2 fusion.74
  131.0 23.3 %collective-permute-done = bf16[2,1,4,80,1536]{4,3,2,1,0:T(8,128)(2,1)S(1)} collective-permute-done((bf16[2,1,4,80,1536]{4,3,2,1,0:T(8,128)(2,1)}, bf16[2,1,4,80,1536]{4,3,2,1,0:T(8,128)(2,1)S(1)}, u32[]{:S(2)}, u32[]{:S(2)}) %collective-permute-start) | collective-permute-done | bytes 1966112 | tf_op jit(solution)/shard_map/while/body/eval_jaxpr/ppermute | solution.py:25
  155.7 2.2 squeeze.24
  157.9 2.9 squeeze.25
  160.8 2.2 fusion.74
  170.8 23.3 %collective-permute-done = bf16[2,1,4,80,1536]{4,3,2,1,0:T(8,128)(2,1)S(1)} collective-permute-done((bf16[2,1,4,80,1536]{4,3,2,1,0:T(8,128)(2,1)}, bf16[2,1,4,80,1536]{4,3,2,1,0:T(8,128)(2,1)S(1)}, u32[]{:S(2)}, u32[]{:S(2)}) %collective-permute-start) | collective-permute-done | bytes 1966112 | tf_op jit(solution)/shard_map/while/body/eval_jaxpr/ppermute | solution.py:25
  195.6 2.2 squeeze.24
  197.8 2.9 squeeze.25
  200.7 2.2 fusion.74
  210.7 23.3 %collective-permute-done = bf16[2,1,4,80,1536]{4,3,2,1,0:T(8,128)(2,1)S(1)} collective-permute-done((bf16[2,1,4,80,1536]{4,3,2,1,0:T(8,128)(2,1)}, bf16[2,1,4,80,1536]{4,3,2,1,0:T(8,128)(2,1)S(1)}, u32[]{:S(2)}, u32[]{:S(2)}) %collective-permute-start) | collective-permute-done | bytes 1966112 | tf_op jit(solution)/shard_map/while/body/eval_jaxpr/ppermute | solution.py:25
  235.5 2.2 squeeze.24
  237.7 2.9 squeeze.25
  240.6 2.2 fusion.74
  250.6 23.3 %collective-permute-done = bf16[2,1,4,80,1536]{4,3,2,1,0:T(8,128)(2,1)S(1)} collective-permute-done((bf16[2,1,4,80,1536]{4,3,2,1,0:T(8,128)(2,1)}, bf16[2,1,4,80,1536]{4,3,2,1,0:T(8,128)(2,1)S(1)}, u32[]{:S(2)}, u32[]{:S(2)}) %collective-permute-start) | collective-permute-done | bytes 1966112 | tf_op jit(solution)/shard_map/while/body/eval_jaxpr/ppermute | solution.py:25
  275.3 2.2 squeeze.24
  277.6 2.9 squeeze.25
  280.5 2.2 fusion.74
  290.5 23.3 %collective-permute-done = bf16[2,1,4,80,1536]{4,3,2,1,0:T(8,128)(2,1)S(1)} collective-permute-done((bf16[2,1,4,80,1536]{4,3,2,1,0:T(8,128)(2,1)}, bf16[2,1,4,80,1536]{4,3,2,1,0:T(8,128)(2,1)S(1)}, u32[]{:S(2)}, u32[]{:S(2)}) %collective-permute-start) | collective-permute-done | bytes 1966112 | tf_op jit(solution)/shard_map/while/body/eval_jaxpr/ppermute | solution.py:25
  315.2 2.2 squeeze.24
  317.5 2.9 squeeze.25
  320.4 2.2 fusion.74
  330.3 23.3 %collective-permute-done = bf16[2,1,4,80,1536]{4,3,2,1,0:T(8,128)(2,1)S(1)} collective-permute-done((bf16[2,1,4,80,1536]{4,3,2,1,0:T(8,128)(2,1)}, bf16[2,1,4,80,1536]{4,3,2,1,0:T(8,128)(2,1)S(1)}, u32[]{:S(2)}, u32[]{:S(2)}) %collective-permute-start) | collective-permute-done | bytes 1966112 | tf_op jit(solution)/shard_map/while/body/eval_jaxpr/ppermute | solution.py:25
  355.1 2.2 squeeze.24
  357.3 2.9 squeeze.25
  360.2 2.2 fusion.74
  370.2 23.3 %collective-permute-done = bf16[2,1,4,80,1536]{4,3,2,1,0:T(8,128)(2,1)S(1)} collective-permute-done((bf16[2,1,4,80,1536]{4,3,2,1,0:T(8,128)(2,1)}, bf16[2,1,4,80,1536]{4,3,2,1,0:T(8,128)(2,1)S(1)}, u32[]{:S(2)}, u32[]{:S(2)}) %collective-permute-start) | collective-permute-done | bytes 1966112 | tf_op jit(solution)/shard_map/while/body/eval_jaxpr/ppermute | solution.py:25
  395.0 2.2 squeeze.24
  397.2 2.9 squeeze.25
  400.1 2.2 fusion.74
  410.1 23.3 %collective-permute-done = bf16[2,1,4,80,1536]{4,3,2,1,0:T(8,128)(2,1)S(1)} collective-permute-done((bf16[2,1,4,80,1536]{4,3,2,1,0:T(8,128)(2,1)}, bf16[2,1,4,80,1536]{4,3,2,1,0:T(8,128)(2,1)S(1)}, u32[]{:S(2)}, u32[]{:S(2)}) %collective-permute-start) | collective-permute-done | bytes 1966112 | tf_op jit(solution)/shard_map/while/body/eval_jaxpr/ppermute | solution.py:25
  437.1 2.9 squeeze.25
  440.0 2.2 fusion.74
  450.0 23.3 %collective-permute-done = bf16[2,1,4,80,1536]{4,3,2,1,0:T(8,128)(2,1)S(1)} collective-permute-done((bf16[2,1,4,80,1536]{4,3,2,1,0:T(8,128)(2,1)}, bf16[2,1,4,80,1536]{4,3,2,1,0:T(8,128)(2,1)S(1)}, u32[]{:S(2)}, u32[]{:S(2)}) %collective-permute-start) | collective-permute-done | bytes 1966112 | tf_op jit(solution)/shard_map/while/body/eval_jaxpr/ppermute | solution.py:25
  474.7 2.2 squeeze.24
  477.0 2.9 squeeze.25
  479.9 2.2 fusion.74
  489.9 23.3 %collective-permute-done = bf16[2,1,4,80,1536]{4,3,2,1,0:T(8,128)(2,1)S(1)} collective-permute-done((bf16[2,1,4,80,1536]{4,3,2,1,0:T(8,128)(2,1)}, bf16[2,1,4,80,1536]{4,3,2,1,0:T(8,128)(2,1)S(1)}, u32[]{:S(2)}, u32[]{:S(2)}) %collective-permute-start) | collective-permute-done | bytes 1966112 | tf_op jit(solution)/shard_map/while/body/eval_jaxpr/ppermute | solution.py:25
  514.6 2.2 squeeze.24
  516.8 2.9 squeeze.25
  519.7 2.2 fusion.74
  529.7 23.3 %collective-permute-done = bf16[2,1,4,80,1536]{4,3,2,1,0:T(8,128)(2,1)S(1)} collective-permute-done((bf16[2,1,4,80,1536]{4,3,2,1,0:T(8,128)(2,1)}, bf16[2,1,4,80,1536]{4,3,2,1,0:T(8,128)(2,1)S(1)}, u32[]{:S(2)}, u32[]{:S(2)}) %collective-permute-start) | collective-permute-done | bytes 1966112 | tf_op jit(solution)/shard_map/while/body/eval_jaxpr/ppermute | solution.py:25
  554.5 2.2 squeeze.24
  556.7 2.9 squeeze.25
  559.6 2.2 fusion.74
  569.6 23.3 %collective-permute-done = bf16[2,1,4,80,1536]{4,3,2,1,0:T(8,128)(2,1)S(1)} collective-permute-done((bf16[2,1,4,80,1536]{4,3,2,1,0:T(8,128)(2,1)}, bf16[2,1,4,80,1536]{4,3,2,1,0:T(8,128)(2,1)S(1)}, u32[]{:S(2)}, u32[]{:S(2)}) %collective-permute-start) | collective-permute-done | bytes 1966112 | tf_op jit(solution)/shard_map/while/body/eval_jaxpr/ppermute | solution.py:25
  596.6 2.9 squeeze.25
  599.5 2.2 fusion.74
  609.5 23.3 %collective-permute-done = bf16[2,1,4,80,1536]{4,3,2,1,0:T(8,128)(2,1)S(1)} collective-permute-done((bf16[2,1,4,80,1536]{4,3,2,1,0:T(8,128)(2,1)}, bf16[2,1,4,80,1536]{4,3,2,1,0:T(8,128)(2,1)S(1)}, u32[]{:S(2)}, u32[]{:S(2)}) %collective-permute-start) | collective-permute-done | bytes 1966112 | tf_op jit(solution)/shard_map/while/body/eval_jaxpr/ppermute | solution.py:25
  634.2 2.2 squeeze.24
  636.5 2.9 squeeze.25
  639.4 2.2 fusion.74
  (336 shorter events, 161.8 us)
Async XLA Ops:
  0.0 35.8 %copy-start.3 = (bf16[1,2,80,1536]{3,2,1,0:T(8,128)(2,1)S(1)}, bf16[1,2,80,1536]{3,2,1,0:T(8,128)(2,1)}, u32[]{:S(2)}) copy-start(bf16[1,2,80,1536]{3,2,1,0:T(8,128)(2,1)} %param.11) | copy-start | bytes 1474564
  0.0 35.8 %copy-start.4 = (bf16[1,2,80,1536]{3,2,1,0:T(8,128)(2,1)S(1)}, bf16[1,2,80,1536]{3,2,1,0:T(8,128)(2,1)}, u32[]{:S(2)}) copy-start(bf16[1,2,80,1536]{3,2,1,0:T(8,128)(2,1)} %param.12) | copy-start | bytes 1474564
  2.3 27.6 %collective-permute-start.1 = (bf16[2,1,1,80,1536]{4,3,2,1,0:T(8,128)(2,1)}, bf16[2,1,1,80,1536]{4,3,2,1,0:T(8,128)(2,1)S(1)}, u32[]{:S(2)}, u32[]{:S(2)}) collective-permute-start(bf16[2,1,1,80,1536]{4,3,2,1,0:T(8,128)(2,1)} %get-tuple-element.402), channel_id=1, source_target_pairs={{0,1},{1,2},{2,3},{3,4},{4,5},{5,6},{6,7},{7,8},{8,9},{9,10},{10,1... | collective-permute-start | bytes 1474568 | tf_op jit(solution)/shard_map/ppermute | solution.py:16
  8.6 27.1 %collective-permute-start.2 = (bf16[2,1,1,80,1536]{4,3,2,1,0:T(8,128)(2,1)S(1)}, bf16[2,1,1,80,1536]{4,3,2,1,0:T(8,128)(2,1)S(1)}, u32[]{:S(2)}, u32[]{:S(2)}) collective-permute-start(bf16[2,1,1,80,1536]{4,3,2,1,0:T(8,128)(2,1)S(1)} %get-tuple-element.403), channel_id=1, source_target_pairs={{1,0},{2,1},{3,2},{4,3},{5,4},{6,5},{7,6},{8,7},{9,8},{10,9},{11,1... | collective-permute-start | bytes 1474568 | tf_op jit(solution)/shard_map/ppermute | solution.py:17
  48.1 26.4 %collective-permute-start = (bf16[2,1,4,80,1536]{4,3,2,1,0:T(8,128)(2,1)}, bf16[2,1,4,80,1536]{4,3,2,1,0:T(8,128)(2,1)S(1)}, u32[]{:S(2)}, u32[]{:S(2)}) collective-permute-start(bf16[2,1,4,80,1536]{4,3,2,1,0:T(8,128)(2,1)} %get-tuple-element.519), channel_id=1, source_target_pairs={{240,0},{0,16},{16,32},{32,48},{48,64},{64,80},{80,96},{96,112},{1... | collective-permute-start | bytes 5898248 | tf_op jit(solution)/shard_map/while/body/eval_jaxpr/ppermute | solution.py:25
  81.1 3.6 copy-start
  81.1 3.7 copy-start.5
  86.4 1.6 copy-start.6
  88.0 26.4 %collective-permute-start = (bf16[2,1,4,80,1536]{4,3,2,1,0:T(8,128)(2,1)}, bf16[2,1,4,80,1536]{4,3,2,1,0:T(8,128)(2,1)S(1)}, u32[]{:S(2)}, u32[]{:S(2)}) collective-permute-start(bf16[2,1,4,80,1536]{4,3,2,1,0:T(8,128)(2,1)} %get-tuple-element.519), channel_id=1, source_target_pairs={{240,0},{0,16},{16,32},{32,48},{48,64},{64,80},{80,96},{96,112},{1... | collective-permute-start | bytes 5898248 | tf_op jit(solution)/shard_map/while/body/eval_jaxpr/ppermute | solution.py:25
  121.0 3.6 copy-start
  121.0 3.7 copy-start.5
  126.3 1.6 copy-start.6
  127.9 26.4 %collective-permute-start = (bf16[2,1,4,80,1536]{4,3,2,1,0:T(8,128)(2,1)}, bf16[2,1,4,80,1536]{4,3,2,1,0:T(8,128)(2,1)S(1)}, u32[]{:S(2)}, u32[]{:S(2)}) collective-permute-start(bf16[2,1,4,80,1536]{4,3,2,1,0:T(8,128)(2,1)} %get-tuple-element.519), channel_id=1, source_target_pairs={{240,0},{0,16},{16,32},{32,48},{48,64},{64,80},{80,96},{96,112},{1... | collective-permute-start | bytes 5898248 | tf_op jit(solution)/shard_map/while/body/eval_jaxpr/ppermute | solution.py:25
  160.8 3.6 copy-start
  160.8 3.7 copy-start.5
  166.1 1.6 copy-start.6
  167.8 26.4 %collective-permute-start = (bf16[2,1,4,80,1536]{4,3,2,1,0:T(8,128)(2,1)}, bf16[2,1,4,80,1536]{4,3,2,1,0:T(8,128)(2,1)S(1)}, u32[]{:S(2)}, u32[]{:S(2)}) collective-permute-start(bf16[2,1,4,80,1536]{4,3,2,1,0:T(8,128)(2,1)} %get-tuple-element.519), channel_id=1, source_target_pairs={{240,0},{0,16},{16,32},{32,48},{48,64},{64,80},{80,96},{96,112},{1... | collective-permute-start | bytes 5898248 | tf_op jit(solution)/shard_map/while/body/eval_jaxpr/ppermute | solution.py:25
  200.7 3.6 copy-start
  200.7 3.7 copy-start.5
  206.0 1.6 copy-start.6
  207.6 26.4 %collective-permute-start = (bf16[2,1,4,80,1536]{4,3,2,1,0:T(8,128)(2,1)}, bf16[2,1,4,80,1536]{4,3,2,1,0:T(8,128)(2,1)S(1)}, u32[]{:S(2)}, u32[]{:S(2)}) collective-permute-start(bf16[2,1,4,80,1536]{4,3,2,1,0:T(8,128)(2,1)} %get-tuple-element.519), channel_id=1, source_target_pairs={{240,0},{0,16},{16,32},{32,48},{48,64},{64,80},{80,96},{96,112},{1... | collective-permute-start | bytes 5898248 | tf_op jit(solution)/shard_map/while/body/eval_jaxpr/ppermute | solution.py:25
  240.6 3.6 copy-start
  240.6 3.7 copy-start.5
  245.9 1.6 copy-start.6
  247.5 26.4 %collective-permute-start = (bf16[2,1,4,80,1536]{4,3,2,1,0:T(8,128)(2,1)}, bf16[2,1,4,80,1536]{4,3,2,1,0:T(8,128)(2,1)S(1)}, u32[]{:S(2)}, u32[]{:S(2)}) collective-permute-start(bf16[2,1,4,80,1536]{4,3,2,1,0:T(8,128)(2,1)} %get-tuple-element.519), channel_id=1, source_target_pairs={{240,0},{0,16},{16,32},{32,48},{48,64},{64,80},{80,96},{96,112},{1... | collective-permute-start | bytes 5898248 | tf_op jit(solution)/shard_map/while/body/eval_jaxpr/ppermute | solution.py:25
  280.5 3.6 copy-start
  280.5 3.7 copy-start.5
  285.8 1.6 copy-start.6
  287.4 26.4 %collective-permute-start = (bf16[2,1,4,80,1536]{4,3,2,1,0:T(8,128)(2,1)}, bf16[2,1,4,80,1536]{4,3,2,1,0:T(8,128)(2,1)S(1)}, u32[]{:S(2)}, u32[]{:S(2)}) collective-permute-start(bf16[2,1,4,80,1536]{4,3,2,1,0:T(8,128)(2,1)} %get-tuple-element.519), channel_id=1, source_target_pairs={{240,0},{0,16},{16,32},{32,48},{48,64},{64,80},{80,96},{96,112},{1... | collective-permute-start | bytes 5898248 | tf_op jit(solution)/shard_map/while/body/eval_jaxpr/ppermute | solution.py:25
  320.4 3.6 copy-start
  320.4 3.7 copy-start.5
  325.6 1.6 copy-start.6
  327.3 26.4 %collective-permute-start = (bf16[2,1,4,80,1536]{4,3,2,1,0:T(8,128)(2,1)}, bf16[2,1,4,80,1536]{4,3,2,1,0:T(8,128)(2,1)S(1)}, u32[]{:S(2)}, u32[]{:S(2)}) collective-permute-start(bf16[2,1,4,80,1536]{4,3,2,1,0:T(8,128)(2,1)} %get-tuple-element.519), channel_id=1, source_target_pairs={{240,0},{0,16},{16,32},{32,48},{48,64},{64,80},{80,96},{96,112},{1... | collective-permute-start | bytes 5898248 | tf_op jit(solution)/shard_map/while/body/eval_jaxpr/ppermute | solution.py:25
  360.2 3.6 copy-start
  360.2 3.7 copy-start.5
  365.5 1.6 copy-start.6
  367.1 26.4 %collective-permute-start = (bf16[2,1,4,80,1536]{4,3,2,1,0:T(8,128)(2,1)}, bf16[2,1,4,80,1536]{4,3,2,1,0:T(8,128)(2,1)S(1)}, u32[]{:S(2)}, u32[]{:S(2)}) collective-permute-start(bf16[2,1,4,80,1536]{4,3,2,1,0:T(8,128)(2,1)} %get-tuple-element.519), channel_id=1, source_target_pairs={{240,0},{0,16},{16,32},{32,48},{48,64},{64,80},{80,96},{96,112},{1... | collective-permute-start | bytes 5898248 | tf_op jit(solution)/shard_map/while/body/eval_jaxpr/ppermute | solution.py:25
  400.1 3.6 copy-start
  400.1 3.7 copy-start.5
  405.4 1.6 copy-start.6
  407.0 26.4 %collective-permute-start = (bf16[2,1,4,80,1536]{4,3,2,1,0:T(8,128)(2,1)}, bf16[2,1,4,80,1536]{4,3,2,1,0:T(8,128)(2,1)S(1)}, u32[]{:S(2)}, u32[]{:S(2)}) collective-permute-start(bf16[2,1,4,80,1536]{4,3,2,1,0:T(8,128)(2,1)} %get-tuple-element.519), channel_id=1, source_target_pairs={{240,0},{0,16},{16,32},{32,48},{48,64},{64,80},{80,96},{96,112},{1... | collective-permute-start | bytes 5898248 | tf_op jit(solution)/shard_map/while/body/eval_jaxpr/ppermute | solution.py:25
  440.0 3.6 copy-start
  440.0 3.7 copy-start.5
  445.3 1.6 copy-start.6
  446.9 26.4 %collective-permute-start = (bf16[2,1,4,80,1536]{4,3,2,1,0:T(8,128)(2,1)}, bf16[2,1,4,80,1536]{4,3,2,1,0:T(8,128)(2,1)S(1)}, u32[]{:S(2)}, u32[]{:S(2)}) collective-permute-start(bf16[2,1,4,80,1536]{4,3,2,1,0:T(8,128)(2,1)} %get-tuple-element.519), channel_id=1, source_target_pairs={{240,0},{0,16},{16,32},{32,48},{48,64},{64,80},{80,96},{96,112},{1... | collective-permute-start | bytes 5898248 | tf_op jit(solution)/shard_map/while/body/eval_jaxpr/ppermute | solution.py:25
  479.9 3.6 copy-start
  479.9 3.7 copy-start.5
  485.2 1.6 copy-start.6
  486.8 26.4 %collective-permute-start = (bf16[2,1,4,80,1536]{4,3,2,1,0:T(8,128)(2,1)}, bf16[2,1,4,80,1536]{4,3,2,1,0:T(8,128)(2,1)S(1)}, u32[]{:S(2)}, u32[]{:S(2)}) collective-permute-start(bf16[2,1,4,80,1536]{4,3,2,1,0:T(8,128)(2,1)} %get-tuple-element.519), channel_id=1, source_target_pairs={{240,0},{0,16},{16,32},{32,48},{48,64},{64,80},{80,96},{96,112},{1... | collective-permute-start | bytes 5898248 | tf_op jit(solution)/shard_map/while/body/eval_jaxpr/ppermute | solution.py:25
  519.7 3.6 copy-start
  519.7 3.7 copy-start.5
  525.0 1.6 copy-start.6
  526.7 26.4 %collective-permute-start = (bf16[2,1,4,80,1536]{4,3,2,1,0:T(8,128)(2,1)}, bf16[2,1,4,80,1536]{4,3,2,1,0:T(8,128)(2,1)S(1)}, u32[]{:S(2)}, u32[]{:S(2)}) collective-permute-start(bf16[2,1,4,80,1536]{4,3,2,1,0:T(8,128)(2,1)} %get-tuple-element.519), channel_id=1, source_target_pairs={{240,0},{0,16},{16,32},{32,48},{48,64},{64,80},{80,96},{96,112},{1... | collective-permute-start | bytes 5898248 | tf_op jit(solution)/shard_map/while/body/eval_jaxpr/ppermute | solution.py:25
  559.6 3.6 copy-start
  559.6 3.7 copy-start.5
  564.9 1.6 copy-start.6
  566.5 26.4 %collective-permute-start = (bf16[2,1,4,80,1536]{4,3,2,1,0:T(8,128)(2,1)}, bf16[2,1,4,80,1536]{4,3,2,1,0:T(8,128)(2,1)S(1)}, u32[]{:S(2)}, u32[]{:S(2)}) collective-permute-start(bf16[2,1,4,80,1536]{4,3,2,1,0:T(8,128)(2,1)} %get-tuple-element.519), channel_id=1, source_target_pairs={{240,0},{0,16},{16,32},{32,48},{48,64},{64,80},{80,96},{96,112},{1... | collective-permute-start | bytes 5898248 | tf_op jit(solution)/shard_map/while/body/eval_jaxpr/ppermute | solution.py:25
  599.5 3.6 copy-start
  599.5 3.7 copy-start.5
  604.8 1.6 copy-start.6
  606.4 26.4 %collective-permute-start = (bf16[2,1,4,80,1536]{4,3,2,1,0:T(8,128)(2,1)}, bf16[2,1,4,80,1536]{4,3,2,1,0:T(8,128)(2,1)S(1)}, u32[]{:S(2)}, u32[]{:S(2)}) collective-permute-start(bf16[2,1,4,80,1536]{4,3,2,1,0:T(8,128)(2,1)} %get-tuple-element.519), channel_id=1, source_target_pairs={{240,0},{0,16},{16,32},{32,48},{48,64},{64,80},{80,96},{96,112},{1... | collective-permute-start | bytes 5898248 | tf_op jit(solution)/shard_map/while/body/eval_jaxpr/ppermute | solution.py:25
  639.4 3.6 copy-start
  639.4 3.7 copy-start.5
  644.7 1.6 copy-start.6
  (2 other events, 2.9 us)
where the time goes:
time: 653 us; the launch traced here: 649 us
  waiting for transfers between devices  367 us (56%)
  local copies, waits for them, and re-layouts  138 us (21%)
  other arithmetic  70 us (11%)
  matrix products  64.3 us (10%)
  starting transfers between devices  8.34 us (1%)
    ppermute x15, waiting for transfers between devices, shifted(): return lax.ppermute(block, axis, route)  349 us
    squeeze x15, local copies, waits for them, and re-layouts, attend(): v_heads = visiting[1].reshape(keys_n, head_count, HEAD_DIM)  43.4 us
    dot_general x16, matrix products, attend(): jnp.einsum('qhd,khd->hqk', q_heads, k_heads, preferred_element_type=jnp.f...  35.8 us
    squeeze x15, local copies, waits for them, and re-layouts, attend(): k_heads = visiting[0].reshape(keys_n, head_count, HEAD_DIM)  33.4 us
    dot_general x16, matrix products, attend(): jnp.einsum('hqk,khd->qhd', weights_low, v_heads, preferred_element_type=j...  28.5 us
    while x120, local copies, waits for them, and re-layouts  24.3 us
    and x16, other arithmetic, attend(): linked[:, :, None, None]  22.5 us
    slice x16, local copies, waits for them, and re-layouts, attend(): v_heads = visiting[1].reshape(keys_n, head_count, HEAD_DIM)  22 us
  transfers between devices with their start and end apart: 17, of which 17 were waited for; matrix products, arithmetic and copies ran while one was open for 8% of the time, Pallas kernels for 0%

commit v1 on v0

v1 whole, which is shorter than its diff:
```python
import functools

import jax
import jax.numpy as jnp
from jax import lax
from jax.experimental import pallas as pl
from jax.experimental.pallas import tpu as pltpu
from jax.sharding import PartitionSpec as P


HEAD_DIM = 128
MESH = pl.DeviceIdType.MESH
NEG = -1e30


def body(frames, pairs, cols, slots, kf_ref, reach_ref, used_ref, q_ref, k_ref, v_ref, o_ref,
         buf_a, buf_b, out_a, out_b, main_send, main_recv, rim_send, rim_recv, out_send, out_recv):
    me = lax.axis_index("frame")
    pair = lax.axis_index("row")
    core = lax.rem(me, 2)
    half = lax.rem(me // 2, 2)
    bufs, outs = (buf_a, buf_b), (out_a, out_b)
    keys = 3 * cols
    two = 2 * cols
    v_at, q_at = keys, 2 * keys
    has_rim = jnp.logical_or(
        jnp.logical_and(half == 1, pair < pairs - 1), jnp.logical_and(half == 0, pair > 0)
    )
    rim_pair = jnp.where(half == 1, pair + 1, pair - 1)
    rim_frame = 4 * (me // 4) + 2 * (1 - half) + core
    rim_row = pl.multiple_of(half * cols, cols)

    def head_of(device, slot):
        return 3 * (device // 4) + (2 * lax.rem(device, 2) if slot == 0 else 1)

    barrier = pltpu.get_barrier_semaphore()

    @pl.loop(1, frames)
    def _(d):
        pl.semaphore_signal(barrier, inc=1, device_id=(lax.rem(me + d, frames), pair), device_id_type=MESH)

    @pl.when(has_rim)
    def _():
        pl.semaphore_signal(barrier, inc=1, device_id=(rim_frame, rim_pair), device_id_type=MESH)
        pl.semaphore_wait(barrier, frames)

    @pl.when(jnp.logical_not(has_rim))
    def _():
        pl.semaphore_wait(barrier, frames - 1)

    def pieces(device, slot):
        buf = bufs[slot]
        col = pl.multiple_of(head_of(device, slot) * HEAD_DIM, HEAD_DIM)
        q_row = pl.multiple_of(lax.rem(device // 2, 2) * cols, cols)
        at = pl.ds(col, HEAD_DIM)
        return (
            (k_ref.at[:, at], buf.at[me, pl.ds(0, two)]),
            (v_ref.at[:, at], buf.at[me, pl.ds(v_at, two)]),
            (q_ref.at[pl.ds(q_row, cols), at], buf.at[me, pl.ds(q_at, cols)]),
        )

    def send_main(device, slot):
        for src, dst in pieces(device, slot):
            pltpu.make_async_remote_copy(
                src_ref=src, dst_ref=dst, send_sem=main_send.at[slot, device], recv_sem=main_recv.at[slot, me],
                device_id=(device, pair), device_id_type=MESH,
            ).start()

    def keep_main(slot):
        for src, dst in pieces(me, slot):
            pltpu.make_async_copy(src, dst, main_recv.at[slot, me]).start()

    def wait_rows(ref, frame, rows, sem):
        view = ref.at[frame, pl.ds(0, rows)]
        pltpu.make_async_copy(view, view, sem).wait()

    keep_main(0)

    @pl.loop(1, frames)
    def _(d):
        send_main(lax.rem(me + d, frames), 0)

    @pl.when(core == 0)
    def _():
        keep_main(1)

    @pl.loop(1, frames)
    def _(d):
        device = lax.rem(me + d, frames)

        @pl.when(lax.rem(device, 2) == 0)
        def _():
            send_main(device, 1)

    def pass_rim(frame, slot):
        buf = bufs[slot]
        wait_rows(buf, frame, 2 * two + cols, main_recv.at[slot, frame])

        @pl.when(has_rim)
        def _():
            for base in (0, v_at):
                pltpu.make_async_remote_copy(
                    src_ref=buf.at[frame, pl.ds(pl.multiple_of(base + rim_row, cols), cols)],
                    dst_ref=buf.at[frame, pl.ds(base + two, cols)],
                    send_sem=rim_send.at[slot, frame], recv_sem=rim_recv.at[slot, frame],
                    device_id=(rim_frame, rim_pair), device_id_type=MESH,
                ).start()

    def clear_rim(slot):
        @pl.when(jnp.logical_not(has_rim))
        def _():
            @pl.loop(0, frames)
            def _(frame):
                for base in (0, v_at):
                    bufs[slot][frame, pl.ds(base + two, cols), :] = jnp.zeros((cols, HEAD_DIM), jnp.bfloat16)

    def wait_rim(slot):
        @pl.when(has_rim)
        def _():
            @pl.loop(0, frames)
            def _(frame):
                wait_rows(bufs[slot], frame, two, rim_recv.at[slot, frame])

    key_row = lax.broadcasted_iota(jnp.int32, (1, keys), 1) // cols
    distance = jnp.where(key_row == half, 0, 1)
    distance = jnp.where(jnp.logical_and(key_row == 2, jnp.logical_not(has_rim)), 9, distance)
    factor = HEAD_DIM ** -0.5 * 1.4426950408889634

    def attend(frame, slot):
        buf = bufs[slot]
        q = buf[frame, pl.ds(q_at, cols), :]
        targets = [kf_ref[j, frame] for j in range(slots)]
        spans = [jnp.where(j < used_ref[frame], reach_ref[j, frame], -1) for j in range(slots)]
        scores = []
        for j in range(slots):
            spread = spans[j]
            for i in range(slots):
                if i != j:
                    same = targets[i] == targets[j]
                    spread = jnp.maximum(spread, jnp.where(same, spans[i], -1))
            for i in range(j):
                spread = jnp.where(jnp.logical_and(targets[i] == targets[j], spans[i] >= 0), -1, spread)
            spread = jnp.where(spans[j] >= 0, spread, -1)
            s = lax.dot_general(
                q, buf[targets[j], pl.ds(0, keys), :], (((1,), (1,)), ((), ())), preferred_element_type=jnp.float32
            )
            scores.append(s * factor + jnp.where(distance <= spread, 0.0, NEG))
        peak = functools.reduce(jnp.maximum, scores)
        peak = jnp.max(peak, axis=1, keepdims=True)
        weights = [jnp.exp2(s - peak) for s in scores]
        total = jnp.sum(functools.reduce(jnp.add, weights), axis=1, keepdims=True)
        mixed = None
        for j in range(slots):
            part = lax.dot_general(
                weights[j].astype(jnp.bfloat16), buf[targets[j], pl.ds(v_at, keys), :],
                (((1,), (0,)), ((), ())), preferred_element_type=jnp.float32,
            )
            mixed = part if mixed is None else mixed + part
        outs[slot][frame] = (mixed / total).astype(jnp.bfloat16)

    def out_view(slot):
        col = pl.multiple_of(head_of(me, slot) * HEAD_DIM, HEAD_DIM)
        return o_ref.at[pl.ds(pl.multiple_of(half * cols, cols), cols), pl.ds(col, HEAD_DIM)]

    def send_out(frame, slot):
        @pl.when(frame == me)
        def _():
            pltpu.make_async_copy(outs[slot].at[frame], out_view(slot), out_recv.at[slot, me]).start()

        @pl.when(frame != me)
        def _():
            pltpu.make_async_remote_copy(
                src_ref=outs[slot].at[frame], dst_ref=out_view(slot),
                send_sem=out_send.at[slot, frame], recv_sem=out_recv.at[slot, me],
                device_id=(frame, pair), device_id_type=MESH,
            ).start()

    clear_rim(0)

    @pl.loop(0, frames)
    def _(d):
        pass_rim(lax.rem(me + frames - d, frames), 0)

    wait_rim(0)

    @pl.loop(0, frames)
    def _(d):
        frame = lax.rem(me + d, frames)
        attend(frame, 0)
        send_out(frame, 0)

        @pl.when(core == 0)
        def _():
            pass_rim(lax.rem(me + frames - d, frames), 1)

    @pl.when(core == 0)
    def _():
        clear_rim(1)
        wait_rim(1)

        @pl.loop(0, frames)
        def _(d):
            frame = lax.rem(me + d, frames)
            attend(frame, 1)
            send_out(frame, 1)

    @pl.loop(0, frames)
    def _(device):
        even = lax.rem(device, 2) == 0
        other = device != me

        @pl.when(other)
        def _():
            wait_rows(buf_a, 0, 2 * two + cols, main_send.at[0, device])
            wait_rows(out_a, 0, cols, out_send.at[0, device])

            @pl.when(even)
            def _():
                wait_rows(buf_b, 0, 2 * two + cols, main_send.at[1, device])

            @pl.when(core == 0)
            def _():
                wait_rows(out_b, 0, cols, out_send.at[1, device])

        @pl.when(has_rim)
        def _():
            wait_rows(buf_a, 0, two, rim_send.at[0, device])

            @pl.when(core == 0)
            def _():
                wait_rows(buf_b, 0, two, rim_send.at[1, device])

        wait_rows(out_a, 0, cols, out_recv.at[0, device])

        @pl.when(even)
        def _():
            wait_rows(out_b, 0, cols, out_recv.at[1, device])


def local(query, key, value, key_frames, reach, used):
    _, rows, cols, features = query.shape
    frames, pairs = lax.axis_size("frame"), lax.axis_size("row")
    slots = key_frames.shape[1]
    flat = (rows * cols, features)
    block = (frames, 7 * cols, HEAD_DIM)
    out_block = (frames, cols, HEAD_DIM)
    smem = pl.BlockSpec(memory_space=pltpu.SMEM)
    hbm = pl.BlockSpec(memory_space=pl.ANY)
    out = pl.pallas_call(
        functools.partial(body, frames, pairs, cols, slots),
        out_shape=jax.ShapeDtypeStruct(flat, jnp.bfloat16),
        in_specs=[smem, smem, smem, hbm, hbm, hbm],
        out_specs=hbm,
        scratch_shapes=[
            pltpu.VMEM(block, jnp.bfloat16),
            pltpu.VMEM(block, jnp.bfloat16),
            pltpu.VMEM(out_block, jnp.bfloat16),
            pltpu.VMEM(out_block, jnp.bfloat16),
        ] + [pltpu.SemaphoreType.DMA((2, frames))] * 6,
        compiler_params=pltpu.CompilerParams(
            collective_id=0, has_side_effects=True, vmem_limit_bytes=40 * 1024 * 1024
        ),
        cost_estimate=pl.CostEstimate(flops=2 * 10**9, bytes_accessed=10**7, transcendentals=10**7),
    )(key_frames.T, reach.T, used, query.reshape(flat), key.reshape(flat), value.reshape(flat))
    return out.reshape(query.shape)


def solution(mesh):
    return jax.shard_map(
        local,
        mesh=mesh,
        in_specs=(
            P("frame", "row", None, None),
            P("frame", "row", None, None),
            P("frame", "row", None, None),
            P(),
            P(),
            P(),
        ),
        out_specs=P("frame", "row", None, None),
        check_vma=False,
    )
```

time: 653 us -> 69.2 us (0.11)
  the two profiles are of different devices: /device:TPU:80 before, /device:TPU:73 now
where the time goes in v1:
time: 69.2 us; the launch traced here: 69 us
  Pallas kernels  64.4 us (93%)
  local copies, waits for them, and re-layouts  4.56 us (7%)
    pallas_call x1, Pallas kernels, local(): pl.pallas_call(functools.partial(body, frames, pairs, cols, slots), out_s...  64.4 us
    unnamed x13, local copies, waits for them, and re-layouts  4.56 us

profile of v1, /device:TPU:73, one launch (start us, length us, event | category | flops | bytes accessed | tf_op | source)
XLA Modules:
  0.0 69.0 jit_solution(9749261852969555678)
XLA Ops:
  0.0 0.0 copy-start.4
  0.0 0.0 copy-start.3
  0.0 0.0 copy-start.5
  0.0 0.7 copy-done.4
  0.7 0.0 copy-done.3
  0.7 0.0 copy-done.5
  0.7 0.0 copy-start
  0.7 1.0 %copy-done = bf16[1,2,80,1536]{3,2,1,0:T(8,128)(2,1)S(1)} copy-done((bf16[1,2,80,1536]{3,2,1,0:T(8,128)(2,1)S(1)}, bf16[1,2,80,1536]{3,2,1,0:T(8,128)(2,1)}, u32[]{:S(2)}) %copy-start) | copy-done | bytes 491544
  1.7 0.0 copy-start.1
  1.7 1.0 %copy-done.1 = bf16[1,2,80,1536]{3,2,1,0:T(8,128)(2,1)S(1)} copy-done((bf16[1,2,80,1536]{3,2,1,0:T(8,128)(2,1)S(1)}, bf16[1,2,80,1536]{3,2,1,0:T(8,128)(2,1)}, u32[]{:S(2)}) %copy-start.1) | copy-done | bytes 491544
  2.8 0.0 copy-start.2
  2.8 1.0 %copy-done.2 = bf16[1,2,80,1536]{3,2,1,0:T(8,128)(2,1)S(1)} copy-done((bf16[1,2,80,1536]{3,2,1,0:T(8,128)(2,1)S(1)}, bf16[1,2,80,1536]{3,2,1,0:T(8,128)(2,1)}, u32[]{:S(2)}) %copy-start.2) | copy-done | bytes 491544
  3.8 64.4 %shard_map.64 = bf16[160,1536]{1,0:T(8,128)(2,1)S(1)} custom-call(s32[4,16]{1,0:T(4,128)S(1)} %bitcast.10, s32[4,16]{1,0:T(4,128)S(1)} %bitcast.11, s32[16]{0:T(128)S(1)} %copy-done.5, bf16[160,1536]{1,0:T(8,128)(2,1)S(1)} %bitcast.7, bf16[160,1536]{1,0:T(8,128)(2,1)S(1)} %bitcast.8, bf16[160,1536]{1,0:T(8,128)(2,1)S(1)} %bitcast.9), custom_call_target="tpu_custom_call" | custom-call | flops 2000000000 | bytes 10000000 | tf_op jit(solution)/shard_map/pallas_call | solution.py:249
  68.2 0.8 %copy.8 = bf16[1,2,80,1536]{3,2,1,0:T(8,128)(2,1)} copy(bf16[1,2,80,1536]{3,2,1,0:T(8,128)(2,1)S(1)} %bitcast.6) | data formatting | bytes 983040
Async XLA Ops:
  0.0 0.7 copy-start.4
  0.0 0.7 %copy-start.3 = (s32[16,4]{0,1:T(4,128)S(1)}, s32[16,4]{0,1:T(4,128)}, u32[]{:S(2)}) copy-start(s32[16,4]{0,1:T(4,128)} %param.9) | copy-start | bytes 772
  0.0 0.7 %copy-start.5 = (s32[16]{0:T(128)S(1)}, s32[16]{0:T(128)}, u32[]{:S(2)}) copy-start(s32[16]{0:T(128)} %used_ref.1) | copy-start | bytes 196
  0.7 1.0 %copy-start = (bf16[1,2,80,1536]{3,2,1,0:T(8,128)(2,1)S(1)}, bf16[1,2,80,1536]{3,2,1,0:T(8,128)(2,1)}, u32[]{:S(2)}) copy-start(bf16[1,2,80,1536]{3,2,1,0:T(8,128)(2,1)} %param.6) | copy-start | bytes 1474564
  1.7 1.0 %copy-start.1 = (bf16[1,2,80,1536]{3,2,1,0:T(8,128)(2,1)S(1)}, bf16[1,2,80,1536]{3,2,1,0:T(8,128)(2,1)}, u32[]{:S(2)}) copy-start(bf16[1,2,80,1536]{3,2,1,0:T(8,128)(2,1)} %param.7) | copy-start | bytes 1474564
  2.8 1.0 %copy-start.2 = (bf16[1,2,80,1536]{3,2,1,0:T(8,128)(2,1)S(1)}, bf16[1,2,80,1536]{3,2,1,0:T(8,128)(2,1)}, u32[]{:S(2)}) copy-start(bf16[1,2,80,1536]{3,2,1,0:T(8,128)(2,1)} %param.8) | copy-start | bytes 1474564

commit v2 on v1

v2 whole, which is shorter than its diff:
```python
import functools

import jax
import jax.numpy as jnp
from jax import lax
from jax.experimental import pallas as pl
from jax.experimental.pallas import tpu as pltpu
from jax.sharding import PartitionSpec as P


HEAD_DIM = 128
MESH = pl.DeviceIdType.MESH
NEG = -1e30


def body(frames, pairs, cols, slots, kf_ref, reach_ref, used_ref, q_ref, k_ref, v_ref, o_ref,
         buf_a, buf_b, out_a, out_b, kv_recv, q_recv, main_send, rim_send, rim_recv, out_send, out_recv):
    me = lax.axis_index("frame")
    pair = lax.axis_index("row")
    core = lax.rem(me, 2)
    half = lax.rem(me // 2, 2)
    bufs, outs = (buf_a, buf_b), (out_a, out_b)
    keys = 3 * cols
    two = 2 * cols
    v_at, q_at = keys, 2 * keys
    has_rim = jnp.logical_or(
        jnp.logical_and(half == 1, pair < pairs - 1), jnp.logical_and(half == 0, pair > 0)
    )
    no_rim = jnp.logical_not(has_rim)
    rim_pair = jnp.where(half == 1, pair + 1, pair - 1)
    rim_frame = 4 * (me // 4) + 2 * (1 - half) + core
    rim_row = pl.multiple_of(half * cols, cols)

    def head_of(device, slot):
        return 3 * (device // 4) + (2 * lax.rem(device, 2) if slot == 0 else 1)

    def chip(step, sign):
        k = step // 2
        distance = k + k // 2 - 2 * (k // 2) * lax.rem(k, 2)
        x = lax.rem(me // 4 + 4 + sign * distance, 4)
        return 4 * x + 2 * lax.rem(half + 1 + step, 2)

    barrier = pltpu.get_barrier_semaphore()

    @pl.loop(1, frames)
    def _(d):
        pl.semaphore_signal(barrier, inc=1, device_id=(lax.rem(me + d, frames), pair), device_id_type=MESH)

    @pl.when(has_rim)
    def _():
        pl.semaphore_signal(barrier, inc=1, device_id=(rim_frame, rim_pair), device_id_type=MESH)

    def kv_pieces(device, slot):
        at = pl.ds(pl.multiple_of(head_of(device, slot) * HEAD_DIM, HEAD_DIM), HEAD_DIM)
        buf = bufs[slot]
        return (
            (k_ref.at[:, at], buf.at[me, pl.ds(0, two)]),
            (v_ref.at[:, at], buf.at[me, pl.ds(v_at, two)]),
        )

    def q_piece(device, slot):
        at = pl.ds(pl.multiple_of(head_of(device, slot) * HEAD_DIM, HEAD_DIM), HEAD_DIM)
        row = pl.multiple_of(lax.rem(device // 2, 2) * cols, cols)
        return q_ref.at[pl.ds(row, cols), at], bufs[slot].at[me, pl.ds(q_at, cols)]

    def keep(slot):
        for src, dst in kv_pieces(me, slot):
            pltpu.make_async_copy(src, dst, kv_recv.at[slot, me]).start()
        src, dst = q_piece(me, slot)
        pltpu.make_async_copy(src, dst, q_recv.at[slot]).start()

    def send(src, dst, slot, recv_sem, device):
        pltpu.make_async_remote_copy(
            src_ref=src, dst_ref=dst, send_sem=main_send.at[slot], recv_sem=recv_sem,
            device_id=(device, pair), device_id_type=MESH,
        ).start()

    def send_kv(device, slot):
        for src, dst in kv_pieces(device, slot):
            send(src, dst, slot, kv_recv.at[slot, me], device)

    def send_q(device, slot):
        src, dst = q_piece(device, slot)
        send(src, dst, slot, q_recv.at[slot], device)

    def settle(view, sem):
        pltpu.make_async_copy(view, view, sem).wait()

    keep(0)

    @pl.when(core == 0)
    def _():
        keep(1)

    @pl.when(has_rim)
    def _():
        pl.semaphore_wait(barrier, frames)

    @pl.when(no_rim)
    def _():
        pl.semaphore_wait(barrier, frames - 1)

    @pl.loop(0, frames // 2)
    def _(step):
        for c in range(2):
            device = chip(step, 1) + c

            @pl.when(device != me)
            def _():
                send_kv(device, 0)
                send_q(device, 0)

    @pl.loop(0, frames // 2)
    def _(step):
        device = chip(step, 1)

        @pl.when(device != me)
        def _():
            send_kv(device, 1)

    @pl.loop(0, frames // 2)
    def _(step):
        device = chip(step, 1)

        @pl.when(device != me)
        def _():
            send_q(device, 1)

    def pass_rim(frame, slot):
        buf = bufs[slot]
        settle(buf.at[frame, pl.ds(0, 2 * two)], kv_recv.at[slot, frame])

        @pl.when(has_rim)
        def _():
            for base in (0, v_at):
                pltpu.make_async_remote_copy(
                    src_ref=buf.at[frame, pl.ds(pl.multiple_of(base + rim_row, cols), cols)],
                    dst_ref=buf.at[frame, pl.ds(base + two, cols)],
                    send_sem=rim_send.at[slot], recv_sem=rim_recv.at[slot],
                    device_id=(rim_frame, rim_pair), device_id_type=MESH,
                ).start()

    def pass_rims(step, slot):
        for c in range(2):
            pass_rim(chip(step, -1) + c, slot)

    def clear_rim(slot):
        @pl.loop(0, frames)
        def _(frame):
            for base in (0, v_at):
                bufs[slot][frame, pl.ds(base + two, cols), :] = jnp.zeros((cols, HEAD_DIM), jnp.bfloat16)

    def wait_rest(slot):
        settle(bufs[slot].at[:, pl.ds(0, cols)], q_recv.at[slot])

        @pl.when(has_rim)
        def _():
            settle(bufs[slot].at[:, pl.ds(0, two)], rim_recv.at[slot])

    key_row = lax.broadcasted_iota(jnp.int32, (1, keys), 1) // cols
    distance = jnp.where(key_row == half, 0, 1)
    distance = jnp.where(jnp.logical_and(key_row == 2, no_rim), 9, distance)
    factor = HEAD_DIM ** -0.5 * 1.4426950408889634

    def spreads(frame):
        targets = [kf_ref[j, frame] for j in range(slots)]
        spans = [jnp.where(j < used_ref[frame], reach_ref[j, frame], -1) for j in range(slots)]
        found = []
        for j in range(slots):
            spread = spans[j]
            for i in range(slots):
                if i != j:
                    spread = jnp.maximum(spread, jnp.where(targets[i] == targets[j], spans[i], -1))
            for i in range(j):
                spread = jnp.where(jnp.logical_and(targets[i] == targets[j], spans[i] >= 0), -1, spread)
            found.append(jnp.where(spans[j] >= 0, spread, -1))
        return targets, found

    def attend(group, slot):
        buf = bufs[slot]
        masks = [spreads(frame) for frame in group]
        scores = [
            [
                lax.dot_general(
                    buf[frame, pl.ds(q_at, cols), :], buf[target, pl.ds(0, keys), :],
                    (((1,), (1,)), ((), ())), preferred_element_type=jnp.float32,
                )
                for target in targets
            ]
            for frame, (targets, _) in zip(group, masks)
        ]
        weights, totals = [], []
        for row, (_, found) in zip(scores, masks):
            row = [s * factor + jnp.where(distance <= spread, 0.0, NEG) for s, spread in zip(row, found)]
            peak = jnp.max(functools.reduce(jnp.maximum, row), axis=1, keepdims=True)
            row = [jnp.exp2(s - peak) for s in row]
            totals.append(jnp.sum(functools.reduce(jnp.add, row), axis=1, keepdims=True))
            weights.append(row)
        mixed = [
            functools.reduce(jnp.add, [
                lax.dot_general(
                    w.astype(jnp.bfloat16), buf[target, pl.ds(v_at, keys), :],
                    (((1,), (0,)), ((), ())), preferred_element_type=jnp.float32,
                )
                for w, target in zip(row, targets)
            ])
            for row, (targets, _) in zip(weights, masks)
        ]
        for frame, value, total in zip(group, mixed, totals):
            outs[slot][frame] = (value / total).astype(jnp.bfloat16)

    out_col = [pl.multiple_of(head_of(me, slot) * HEAD_DIM, HEAD_DIM) for slot in range(2)]
    out_row = pl.multiple_of(half * cols, cols)

    def send_out(frame, slot):
        view = o_ref.at[pl.ds(out_row, cols), pl.ds(out_col[slot], HEAD_DIM)]

        @pl.when(frame == me)
        def _():
            pltpu.make_async_copy(outs[slot].at[frame], view, out_recv.at[slot]).start()

        @pl.when(frame != me)
        def _():
            pltpu.make_async_remote_copy(
                src_ref=outs[slot].at[frame], dst_ref=view, send_sem=out_send.at[slot], recv_sem=out_recv.at[slot],
                device_id=(frame, pair), device_id_type=MESH,
            ).start()

    def work(step, slot):
        group = [lax.rem(me + 4 * step + u, frames) for u in range(4)]
        attend(group, slot)
        for frame in group:
            send_out(frame, slot)

    @pl.when(no_rim)
    def _():
        clear_rim(0)
        clear_rim(1)

    @pl.loop(0, frames // 2)
    def _(step):
        pass_rims(step, 0)

    wait_rest(0)

    @pl.loop(0, frames // 4)
    def _(step):
        work(step, 0)

        @pl.when(core == 0)
        def _():
            for i in range(2):
                pass_rims(2 * step + i, 1)

    @pl.when(core == 0)
    def _():
        wait_rest(1)

        @pl.loop(0, frames // 4)
        def _(step):
            work(step, 1)

    settle(buf_a.at[pl.ds(0, frames - 1), pl.ds(0, 2 * two + cols)], main_send.at[0])
    settle(out_a.at[pl.ds(0, frames - 1)], out_send.at[0])

    @pl.when(has_rim)
    def _():
        settle(buf_a.at[:, pl.ds(0, two)], rim_send.at[0])

    @pl.when(core == 0)
    def _():
        settle(buf_b.at[pl.ds(0, frames // 2 - 1), pl.ds(0, 2 * two + cols)], main_send.at[1])
        settle(out_b.at[pl.ds(0, frames - 1)], out_send.at[1])

        @pl.when(has_rim)
        def _():
            settle(buf_b.at[:, pl.ds(0, two)], rim_send.at[1])

    @pl.when(core == 1)
    def _():
        settle(buf_b.at[pl.ds(0, frames // 2), pl.ds(0, 2 * two + cols)], main_send.at[1])

    settle(out_a, out_recv.at[0])
    settle(out_b.at[pl.ds(0, frames // 2)], out_recv.at[1])


def local(query, key, value, key_frames, reach, used):
    _, rows, cols, features = query.shape
    frames, pairs = lax.axis_size("frame"), lax.axis_size("row")
    slots = key_frames.shape[1]
    flat = (rows * cols, features)
    block = (frames, 7 * cols, HEAD_DIM)
    out_block = (frames, cols, HEAD_DIM)
    smem = pl.BlockSpec(memory_space=pltpu.SMEM)
    hbm = pl.BlockSpec(memory_space=pl.ANY)
    out = pl.pallas_call(
        functools.partial(body, frames, pairs, cols, slots),
        out_shape=jax.ShapeDtypeStruct(flat, jnp.bfloat16),
        in_specs=[smem, smem, smem, hbm, hbm, hbm],
        out_specs=hbm,
        scratch_shapes=[
            pltpu.VMEM(block, jnp.bfloat16),
            pltpu.VMEM(block, jnp.bfloat16),
            pltpu.VMEM(out_block, jnp.bfloat16),
            pltpu.VMEM(out_block, jnp.bfloat16),
            pltpu.SemaphoreType.DMA((2, frames)),
        ] + [pltpu.SemaphoreType.DMA((2,))] * 6,
        compiler_params=pltpu.CompilerParams(
            collective_id=0, has_side_effects=True, vmem_limit_bytes=60 * 1024 * 1024
        ),
        cost_estimate=pl.CostEstimate(flops=2 * 10**9, bytes_accessed=10**7, transcendentals=10**7),
    )(key_frames.T, reach.T, used, query.reshape(flat), key.reshape(flat), value.reshape(flat))
    return out.reshape(query.shape)


def solution(mesh):
    return jax.shard_map(
        local,
        mesh=mesh,
        in_specs=(
            P("frame", "row", None, None),
            P("frame", "row", None, None),
            P("frame", "row", None, None),
            P(),
            P(),
            P(),
        ),
        out_specs=P("frame", "row", None, None),
        check_vma=False,
    )
```

time: 69.2 us -> 54 us (0.78)
  the two profiles are of different devices: /device:TPU:73 before, /device:TPU:25 now
where the time goes in v2:
time: 54 us; the launch traced here: 53.9 us
  Pallas kernels  52 us (96%)
  local copies, waits for them, and re-layouts  1.84 us (3%)
    pallas_call x1, Pallas kernels, local(): pl.pallas_call(functools.partial(body, frames, pairs, cols, slots), out_s...  52 us
    unnamed x1, local copies, waits for them, and re-layouts  1.84 us

profile of v2, /device:TPU:25, one launch (start us, length us, event | category | flops | bytes accessed | tf_op | source)
XLA Modules:
  0.0 53.9 jit_solution(12686501694712005847)
XLA Ops:
  0.0 52.0 %shard_map.64 = bf16[160,1536]{1,0:T(8,128)(2,1)} custom-call(s32[4,16]{1,0:T(4,128)} %bitcast.10, s32[4,16]{1,0:T(4,128)} %bitcast.11, s32[16]{0:T(128)} %used_ref.1, bf16[160,1536]{1,0:T(8,128)(2,1)} %bitcast.7, bf16[160,1536]{1,0:T(8,128)(2,1)} %bitcast.8, bf16[160,1536]{1,0:T(8,128)(2,1)} %bitcast.9), custom_call_target="tpu_custom_call" | custom-call | flops 2000000000 | bytes 10000000 | tf_op jit(solution)/shard_map/pallas_call | solution.py:296
  52.0 1.8 %copy.8 = bf16[1,2,80,1536]{3,2,1,0:T(8,128)(2,1)} copy(bf16[1,2,80,1536]{3,2,1,0:T(8,128)(2,1)} %bitcast.6) | data formatting | bytes 983040

commit v3 on v2

--- a/solution.py
+++ b/solution.py
@@ -14,7 +14,7 @@
 
 
 def body(frames, pairs, cols, slots, kf_ref, reach_ref, used_ref, q_ref, k_ref, v_ref, o_ref,
-         buf_a, buf_b, out_a, out_b, kv_recv, q_recv, main_send, rim_send, rim_recv, out_send, out_recv):
+         buf_a, buf_b, out_a, out_b, near_recv, far_recv, main_send, rim_send, rim_recv, out_send, out_recv):
     me = lax.axis_index("frame")
     pair = lax.axis_index("row")
     core = lax.rem(me, 2)
@@ -50,38 +50,40 @@
     def _():
         pl.semaphore_signal(barrier, inc=1, device_id=(rim_frame, rim_pair), device_id_type=MESH)
 
-    def kv_pieces(device, slot):
-        at = pl.ds(pl.multiple_of(head_of(device, slot) * HEAD_DIM, HEAD_DIM), HEAD_DIM)
-        buf = bufs[slot]
+    def piece(ref, device, slot, row, at):
+        lanes = pl.ds(pl.multiple_of(head_of(device, slot) * HEAD_DIM, HEAD_DIM), HEAD_DIM)
         return (
-            (k_ref.at[:, at], buf.at[me, pl.ds(0, two)]),
-            (v_ref.at[:, at], buf.at[me, pl.ds(v_at, two)]),
+            ref.at[pl.ds(pl.multiple_of(row * cols, cols), cols), lanes],
+            bufs[slot].at[me, pl.ds(pl.multiple_of(at * cols, cols), cols)],
         )
 
-    def q_piece(device, slot):
-        at = pl.ds(pl.multiple_of(head_of(device, slot) * HEAD_DIM, HEAD_DIM), HEAD_DIM)
-        row = pl.multiple_of(lax.rem(device // 2, 2) * cols, cols)
-        return q_ref.at[pl.ds(row, cols), at], bufs[slot].at[me, pl.ds(q_at, cols)]
+    def half_of(device):
+        return lax.rem(device // 2, 2)
+
+    def near(device, slot):
+        row = half_of(device)
+        return piece(k_ref, device, slot, row, row), piece(v_ref, device, slot, row, 3 + row)
+
+    def far(device, slot):
+        row = 1 - half_of(device)
+        return (
+            piece(k_ref, device, slot, row, row),
+            piece(v_ref, device, slot, row, 3 + row),
+            piece(q_ref, device, slot, 1 - row, 6),
+        )
 
     def keep(slot):
-        for src, dst in kv_pieces(me, slot):
-            pltpu.make_async_copy(src, dst, kv_recv.at[slot, me]).start()
-        src, dst = q_piece(me, slot)
-        pltpu.make_async_copy(src, dst, q_recv.at[slot]).start()
-
-    def send(src, dst, slot, recv_sem, device):
-        pltpu.make_async_remote_copy(
-            src_ref=src, dst_ref=dst, send_sem=main_send.at[slot], recv_sem=recv_sem,
-            device_id=(device, pair), device_id_type=MESH,
-        ).start()
-
-    def send_kv(device, slot):
-        for src, dst in kv_pieces(device, slot):
-            send(src, dst, slot, kv_recv.at[slot, me], device)
-
-    def send_q(device, slot):
-        src, dst = q_piece(device, slot)
-        send(src, dst, slot, q_recv.at[slot], device)
+        for src, dst in near(me, slot):
+            pltpu.make_async_copy(src, dst, near_recv.at[slot, me]).start()
+        for src, dst in far(me, slot):
+            pltpu.make_async_copy(src, dst, far_recv.at[slot]).start()
+
+    def send(pieces, slot, recv_sem, device):
+        for src, dst in pieces:
+            pltpu.make_async_remote_copy(
+                src_ref=src, dst_ref=dst, send_sem=main_send.at[slot], recv_sem=recv_sem,
+                device_id=(device, pair), device_id_type=MESH,
+            ).start()
 
     def settle(view, sem):
         pltpu.make_async_copy(view, view, sem).wait()
@@ -100,35 +102,24 @@
     def _():
         pl.semaphore_wait(barrier, frames - 1)
 
-    @pl.loop(0, frames // 2)
-    def _(step):
-        for c in range(2):
-            device = chip(step, 1) + c
-
-            @pl.when(device != me)
-            def _():
-                send_kv(device, 0)
-                send_q(device, 0)
-
-    @pl.loop(0, frames // 2)
-    def _(step):
-        device = chip(step, 1)
-
-        @pl.when(device != me)
-        def _():
-            send_kv(device, 1)
-
-    @pl.loop(0, frames // 2)
-    def _(step):
-        device = chip(step, 1)
-
-        @pl.when(device != me)
-        def _():
-            send_q(device, 1)
+    def each(slot, act):
+        @pl.loop(0, frames // 2)
+        def _(step):
+            for c in range(2 - slot):
+                device = chip(step, 1) + c
+
+                @pl.when(device != me)
+                def _():
+                    act(device)
+
+    for slot in range(2):
+        each(slot, lambda device: send(near(device, slot), slot, near_recv.at[slot, me], device))
+    for slot in range(2):
+        each(slot, lambda device: send(far(device, slot), slot, far_recv.at[slot], device))
 
     def pass_rim(frame, slot):
         buf = bufs[slot]
-        settle(buf.at[frame, pl.ds(0, 2 * two)], kv_recv.at[slot, frame])
+        settle(buf.at[frame, pl.ds(0, two)], near_recv.at[slot, frame])
 
         @pl.when(has_rim)
         def _():
@@ -151,7 +142,7 @@
                 bufs[slot][frame, pl.ds(base + two, cols), :] = jnp.zeros((cols, HEAD_DIM), jnp.bfloat16)
 
     def wait_rest(slot):
-        settle(bufs[slot].at[:, pl.ds(0, cols)], q_recv.at[slot])
+        settle(bufs[slot].at[:, pl.ds(0, keys)], far_recv.at[slot])
 
         @pl.when(has_rim)
         def _():
@@ -241,16 +232,17 @@
     def _(step):
         pass_rims(step, 0)
 
+    @pl.when(core == 0)
+    def _():
+        @pl.loop(0, frames // 2)
+        def _(step):
+            pass_rims(step, 1)
+
     wait_rest(0)
 
     @pl.loop(0, frames // 4)
     def _(step):
         work(step, 0)
-
-        @pl.when(core == 0)
-        def _():
-            for i in range(2):
-                pass_rims(2 * step + i, 1)
 
     @pl.when(core == 0)
     def _():

time: 54 us -> 48.4 us (0.90)
  Pallas kernels: 52 us -> 46.5 us
    pallas_call x1, Pallas kernels: 52 us -> 46.5 us  [local(): pl.pallas_call(functools.partial(body, frames, pairs, cols, slots), out_s...]
where the time goes in v3:
time: 48.4 us; the launch traced here: 48.3 us
  Pallas kernels  46.5 us (96%)
  local copies, waits for them, and re-layouts  1.84 us (4%)
    pallas_call x1, Pallas kernels, local(): pl.pallas_call(functools.partial(body, frames, pairs, cols, slots), out_s...  46.5 us
    unnamed x1, local copies, waits for them, and re-layouts  1.84 us

profile of v3, /device:TPU:25, one launch (start us, length us, event | category | flops | bytes accessed | tf_op | source)
XLA Modules:
  0.0 48.3 jit_solution(5576296167848848083)
XLA Ops:
  0.0 46.5 %shard_map.64 = bf16[160,1536]{1,0:T(8,128)(2,1)} custom-call(s32[4,16]{1,0:T(4,128)} %bitcast.10, s32[4,16]{1,0:T(4,128)} %bitcast.11, s32[16]{0:T(128)} %used_ref.1, bf16[160,1536]{1,0:T(8,128)(2,1)} %bitcast.7, bf16[160,1536]{1,0:T(8,128)(2,1)} %bitcast.8, bf16[160,1536]{1,0:T(8,128)(2,1)} %bitcast.9), custom_call_target="tpu_custom_call" | custom-call | flops 2000000000 | bytes 10000000 | tf_op jit(solution)/shard_map/pallas_call | solution.py:288
  46.5 1.8 %copy.8 = bf16[1,2,80,1536]{3,2,1,0:T(8,128)(2,1)} copy(bf16[1,2,80,1536]{3,2,1,0:T(8,128)(2,1)} %bitcast.6) | data formatting | bytes 983040

commit v4 on v3

--- a/solution.py
+++ b/solution.py
@@ -11,6 +11,7 @@
 HEAD_DIM = 128
 MESH = pl.DeviceIdType.MESH
 NEG = -1e30
+GROUP = 8
 
 
 def body(frames, pairs, cols, slots, kf_ref, reach_ref, used_ref, q_ref, k_ref, v_ref, o_ref,
@@ -102,20 +103,28 @@
     def _():
         pl.semaphore_wait(barrier, frames - 1)
 
-    def each(slot, act):
-        @pl.loop(0, frames // 2)
+    steps = frames // 2
+
+    def send_near(step, slot):
+        for c in range(2 - slot):
+            device = chip(step, 1) + c
+
+            @pl.when(device != me)
+            def _():
+                send(near(device, slot), slot, near_recv.at[slot, me], device)
+
+    def send_far(step, slot):
+        for c in range(2 - slot):
+            device = chip(step, 1) + c
+
+            @pl.when(device != me)
+            def _():
+                send(far(device, slot), slot, far_recv.at[slot], device)
+
+    for slot in range(2):
+        @pl.loop(0, steps)
         def _(step):
-            for c in range(2 - slot):
-                device = chip(step, 1) + c
-
-                @pl.when(device != me)
-                def _():
-                    act(device)
-
-    for slot in range(2):
-        each(slot, lambda device: send(near(device, slot), slot, near_recv.at[slot, me], device))
-    for slot in range(2):
-        each(slot, lambda device: send(far(device, slot), slot, far_recv.at[slot], device))
+            send_near(step, slot)
 
     def pass_rim(frame, slot):
         buf = bufs[slot]
@@ -217,40 +226,46 @@
                 device_id=(frame, pair), device_id_type=MESH,
             ).start()
 
-    def work(step, slot):
-        group = [lax.rem(me + 4 * step + u, frames) for u in range(4)]
-        attend(group, slot)
-        for frame in group:
-            send_out(frame, slot)
+    def group_of(step):
+        return [lax.rem(me + GROUP * step + u, frames) for u in range(GROUP)]
 
     @pl.when(no_rim)
     def _():
         clear_rim(0)
         clear_rim(1)
 
-    @pl.loop(0, frames // 2)
+    @pl.loop(0, steps)
     def _(step):
         pass_rims(step, 0)
+        send_far(step, 0)
+
+    @pl.loop(0, steps)
+    def _(step):
+        send_far(step, 1)
+
+        @pl.when(core == 0)
+        def _():
+            pass_rims(step, 1)
+
+    wait_rest(0)
+
+    @pl.loop(0, frames // GROUP)
+    def _(step):
+        attend(group_of(step), 0)
+
+    @pl.loop(0, frames)
+    def _(step):
+        send_out(lax.rem(me + step, frames), 0)
 
     @pl.when(core == 0)
     def _():
-        @pl.loop(0, frames // 2)
+        wait_rest(1)
+
+        @pl.loop(0, frames // GROUP)
         def _(step):
-            pass_rims(step, 1)
-
-    wait_rest(0)
-
-    @pl.loop(0, frames // 4)
-    def _(step):
-        work(step, 0)
-
-    @pl.when(core == 0)
-    def _():
-        wait_rest(1)
-
-        @pl.loop(0, frames // 4)
-        def _(step):
-            work(step, 1)
+            attend(group_of(step), 1)
+            for frame in group_of(step):
+                send_out(frame, 1)
 
     settle(buf_a.at[pl.ds(0, frames - 1), pl.ds(0, 2 * two + cols)], main_send.at[0])
     settle(out_a.at[pl.ds(0, frames - 1)], out_send.at[0])
@@ -298,7 +313,7 @@
             pltpu.SemaphoreType.DMA((2, frames)),
         ] + [pltpu.SemaphoreType.DMA((2,))] * 6,
         compiler_params=pltpu.CompilerParams(
-            collective_id=0, has_side_effects=True, vmem_limit_bytes=60 * 1024 * 1024
+            collective_id=0, has_side_effects=True, vmem_limit_bytes=53 * 1024 * 1024
         ),
         cost_estimate=pl.CostEstimate(flops=2 * 10**9, bytes_accessed=10**7, transcendentals=10**7),
     )(key_frames.T, reach.T, used, query.reshape(flat), key.reshape(flat), value.reshape(flat))

time: 48.4 us -> 47.1 us (0.973)
  Pallas kernels: 46.5 us -> 45.5 us
    pallas_call x1, Pallas kernels: 46.5 us -> 45.5 us  [local(): pl.pallas_call(functools.partial(body, frames, pairs, cols, slots), out_s...]
    unnamed x1 -> x7, local copies, waits for them, and re-layouts: 1.84 us -> 1.48 us
where the time goes in v4:
time: 47.1 us; the launch traced here: 47 us
  Pallas kernels  45.5 us (97%)
  local copies, waits for them, and re-layouts  1.48 us (3%)
    pallas_call x1, Pallas kernels, local(): pl.pallas_call(functools.partial(body, frames, pairs, cols, slots), out_s...  45.5 us
    unnamed x7, local copies, waits for them, and re-layouts  1.48 us

profile of v4, /device:TPU:25, one launch (start us, length us, event | category | flops | bytes accessed | tf_op | source)
XLA Modules:
  0.0 47.0 jit_solution(2016354188644411766)
XLA Ops:
  0.0 0.0 copy-start.1
  0.0 0.0 copy-start
  0.0 0.0 copy-start.2
  0.0 0.7 %copy-done.1 = s32[16,4]{0,1:T(4,128)S(1)} copy-done((s32[16,4]{0,1:T(4,128)S(1)}, s32[16,4]{0,1:T(4,128)}, u32[]{:S(2)}) %copy-start.1) | copy-done | bytes 280
  0.7 0.0 copy-done
  0.7 0.0 copy-done.2
  0.7 45.5 %shard_map.64 = bf16[160,1536]{1,0:T(8,128)(2,1)S(1)} custom-call(s32[4,16]{1,0:T(4,128)S(1)} %bitcast.7, s32[4,16]{1,0:T(4,128)S(1)} %bitcast.8, s32[16]{0:T(128)S(1)} %copy-done.2, bf16[160,1536]{1,0:T(8,128)(2,1)} %bitcast.9, bf16[160,1536]{1,0:T(8,128)(2,1)} %bitcast.10, bf16[160,1536]{1,0:T(8,128)(2,1)} %bitcast.11), custom_call_target="tpu_custom_call" | custom-call | flops 2000000000 | bytes 10000000 | tf_op jit(solution)/shard_map/pallas_call | solution.py:303
  46.2 0.8 %copy.8 = bf16[1,2,80,1536]{3,2,1,0:T(8,128)(2,1)} copy(bf16[1,2,80,1536]{3,2,1,0:T(8,128)(2,1)S(1)} %bitcast.6) | data formatting | bytes 983040
Async XLA Ops:
  0.0 0.7 %copy-start.1 = (s32[16,4]{0,1:T(4,128)S(1)}, s32[16,4]{0,1:T(4,128)}, u32[]{:S(2)}) copy-start(s32[16,4]{0,1:T(4,128)} %param.10) | copy-start | bytes 772
  0.0 0.7 %copy-start = (s32[16,4]{0,1:T(4,128)S(1)}, s32[16,4]{0,1:T(4,128)}, u32[]{:S(2)}) copy-start(s32[16,4]{0,1:T(4,128)} %param.9) | copy-start | bytes 772
  0.0 0.7 %copy-start.2 = (s32[16]{0:T(128)S(1)}, s32[16]{0:T(128)}, u32[]{:S(2)}) copy-start(s32[16]{0:T(128)} %used_ref.1) | copy-start | bytes 196

commit v5 on v4

--- a/solution.py
+++ b/solution.py
@@ -11,11 +11,11 @@
 HEAD_DIM = 128
 MESH = pl.DeviceIdType.MESH
 NEG = -1e30
-GROUP = 8
-
-
-def body(frames, pairs, cols, slots, kf_ref, reach_ref, used_ref, q_ref, k_ref, v_ref, o_ref,
-         buf_a, buf_b, out_a, out_b, near_recv, far_recv, main_send, rim_send, rim_recv, out_send, out_recv):
+GROUPS = (8, 4)
+
+
+def body(frames, pairs, cols, slots, kf_hbm, reach_hbm, used_hbm, q_ref, k_ref, v_ref, o_ref,
+         buf_a, buf_b, out_a, out_b, near_recv, far_recv, main_send, rim_send, rim_recv, out_send, out_recv, kf_ref, reach_ref, used_ref, mask_sem):
     me = lax.axis_index("frame")
     pair = lax.axis_index("row")
     core = lax.rem(me, 2)
@@ -40,6 +40,13 @@
         distance = k + k // 2 - 2 * (k // 2) * lax.rem(k, 2)
         x = lax.rem(me // 4 + 4 + sign * distance, 4)
         return 4 * x + 2 * lax.rem(half + 1 + step, 2)
+
+    mask_copies = [
+        pltpu.make_async_copy(src, dst, mask_sem.at[i])
+        for i, (src, dst) in enumerate(((kf_hbm, kf_ref), (reach_hbm, reach_ref), (used_hbm, used_ref)))
+    ]
+    for copy in mask_copies:
+        copy.start()
 
     barrier = pltpu.get_barrier_semaphore()
 
@@ -226,8 +233,13 @@
                 device_id=(frame, pair), device_id_type=MESH,
             ).start()
 
-    def group_of(step):
-        return [lax.rem(me + GROUP * step + u, frames) for u in range(GROUP)]
+    def group_of(step, size):
+        group = []
+        for u in range(size // 2):
+            t = size // 2 * step + u
+            first = chip(6 - 4 * lax.rem(t, 2) - 2 * (lax.rem(t, 4) // 2) + t // 4, 1)
+            group += [first, first + 1]
+        return group
 
     @pl.when(no_rim)
     def _():
@@ -247,24 +259,29 @@
         def _():
             pass_rims(step, 1)
 
+    for copy in mask_copies:
+        copy.wait()
+
     wait_rest(0)
 
-    @pl.loop(0, frames // GROUP)
+    @pl.loop(0, frames // GROUPS[0])
     def _(step):
-        attend(group_of(step), 0)
-
-    @pl.loop(0, frames)
+        attend(group_of(step, GROUPS[0]), 0)
+
+    @pl.loop(0, steps)
     def _(step):
-        send_out(lax.rem(me + step, frames), 0)
+        for frame in group_of(step, 2):
+            send_out(frame, 0)
 
     @pl.when(core == 0)
     def _():
         wait_rest(1)
 
-        @pl.loop(0, frames // GROUP)
+        @pl.loop(0, frames // GROUPS[1])
         def _(step):
-            attend(group_of(step), 1)
-            for frame in group_of(step):
+            group = group_of(step, GROUPS[1])
+            attend(group, 1)
+            for frame in group:
                 send_out(frame, 1)
 
     settle(buf_a.at[pl.ds(0, frames - 1), pl.ds(0, 2 * two + cols)], main_send.at[0])
@@ -298,12 +315,11 @@
     flat = (rows * cols, features)
     block = (frames, 7 * cols, HEAD_DIM)
     out_block = (frames, cols, HEAD_DIM)
-    smem = pl.BlockSpec(memory_space=pltpu.SMEM)
     hbm = pl.BlockSpec(memory_space=pl.ANY)
     out = pl.pallas_call(
         functools.partial(body, frames, pairs, cols, slots),
         out_shape=jax.ShapeDtypeStruct(flat, jnp.bfloat16),
-        in_specs=[smem, smem, smem, hbm, hbm, hbm],
+        in_specs=[hbm] * 6,
         out_specs=hbm,
         scratch_shapes=[
             pltpu.VMEM(block, jnp.bfloat16),
@@ -311,7 +327,12 @@
             pltpu.VMEM(out_block, jnp.bfloat16),
             pltpu.VMEM(out_block, jnp.bfloat16),
             pltpu.SemaphoreType.DMA((2, frames)),
-        ] + [pltpu.SemaphoreType.DMA((2,))] * 6,
+        ] + [pltpu.SemaphoreType.DMA((2,))] * 6 + [
+            pltpu.SMEM((slots, frames), jnp.int32),
+            pltpu.SMEM((slots, frames), jnp.int32),
+            pltpu.SMEM((frames,), jnp.int32),
+            pltpu.SemaphoreType.DMA((3,)),
+        ],
         compiler_params=pltpu.CompilerParams(
             collective_id=0, has_side_effects=True, vmem_limit_bytes=53 * 1024 * 1024
         ),

time: 47.1 us -> 45.7 us (0.970)
  Pallas kernels: 45.5 us -> 44.1 us
    pallas_call x1, Pallas kernels: 45.5 us -> 44.1 us  [local(): pl.pallas_call(functools.partial(body, frames, pairs, cols, slots), out_s...]
where the time goes in v5:
time: 45.7 us; the launch traced here: 45.6 us
  Pallas kernels  44.1 us (96%)
  local copies, waits for them, and re-layouts  1.48 us (3%)
    pallas_call x1, Pallas kernels, local(): pl.pallas_call(functools.partial(body, frames, pairs, cols, slots), out_s...  44.1 us
    unnamed x7, local copies, waits for them, and re-layouts  1.48 us

profile of v5, /device:TPU:25, one launch (start us, length us, event | category | flops | bytes accessed | tf_op | source)
XLA Modules:
  0.0 45.6 jit_solution(10169574047207912531)
XLA Ops:
  0.0 0.0 copy-start.1
  0.0 0.0 copy-start
  0.0 0.0 copy-start.2
  0.0 0.7 %copy-done.1 = s32[16,4]{0,1:T(4,128)S(1)} copy-done((s32[16,4]{0,1:T(4,128)S(1)}, s32[16,4]{0,1:T(4,128)}, u32[]{:S(2)}) %copy-start.1) | copy-done | bytes 280
  0.7 0.0 copy-done
  0.7 0.0 copy-done.2
  0.7 44.1 %shard_map.64 = bf16[160,1536]{1,0:T(8,128)(2,1)S(1)} custom-call(s32[4,16]{1,0:T(4,128)S(1)} %bitcast.7, s32[4,16]{1,0:T(4,128)S(1)} %bitcast.8, s32[16]{0:T(128)S(1)} %copy-done.2, bf16[160,1536]{1,0:T(8,128)(2,1)} %bitcast.9, bf16[160,1536]{1,0:T(8,128)(2,1)} %bitcast.10, bf16[160,1536]{1,0:T(8,128)(2,1)} %bitcast.11), custom_call_target="tpu_custom_call" | custom-call | flops 2000000000 | bytes 10000000 | tf_op jit(solution)/shard_map/pallas_call | solution.py:319
  44.8 0.8 %copy.8 = bf16[1,2,80,1536]{3,2,1,0:T(8,128)(2,1)} copy(bf16[1,2,80,1536]{3,2,1,0:T(8,128)(2,1)S(1)} %bitcast.6) | data formatting | bytes 983040
Async XLA Ops:
  0.0 0.7 %copy-start.1 = (s32[16,4]{0,1:T(4,128)S(1)}, s32[16,4]{0,1:T(4,128)}, u32[]{:S(2)}) copy-start(s32[16,4]{0,1:T(4,128)} %param.10) | copy-start | bytes 772
  0.0 0.7 %copy-start = (s32[16,4]{0,1:T(4,128)S(1)}, s32[16,4]{0,1:T(4,128)}, u32[]{:S(2)}) copy-start(s32[16,4]{0,1:T(4,128)} %param.9) | copy-start | bytes 772
  0.0 0.7 %copy-start.2 = (s32[16]{0:T(128)S(1)}, s32[16]{0:T(128)}, u32[]{:S(2)}) copy-start(s32[16]{0:T(128)} %used_hbm.1) | copy-start | bytes 196

commit v6 on v5

--- a/solution.py
+++ b/solution.py
@@ -23,14 +23,14 @@
     bufs, outs = (buf_a, buf_b), (out_a, out_b)
     keys = 3 * cols
     two = 2 * cols
-    v_at, q_at = keys, 2 * keys
+    q_at = 2 * keys
     has_rim = jnp.logical_or(
         jnp.logical_and(half == 1, pair < pairs - 1), jnp.logical_and(half == 0, pair > 0)
     )
     no_rim = jnp.logical_not(has_rim)
     rim_pair = jnp.where(half == 1, pair + 1, pair - 1)
     rim_frame = 4 * (me // 4) + 2 * (1 - half) + core
-    rim_row = pl.multiple_of(half * cols, cols)
+    rim_row = pl.multiple_of(half * two, two)
 
     def head_of(device, slot):
         return 3 * (device // 4) + (2 * lax.rem(device, 2) if slot == 0 else 1)
@@ -70,13 +70,13 @@
 
     def near(device, slot):
         row = half_of(device)
-        return piece(k_ref, device, slot, row, row), piece(v_ref, device, slot, row, 3 + row)
+        return piece(k_ref, device, slot, row, 2 * row), piece(v_ref, device, slot, row, 2 * row + 1)
 
     def far(device, slot):
         row = 1 - half_of(device)
         return (
-            piece(k_ref, device, slot, row, row),
-            piece(v_ref, device, slot, row, 3 + row),
+            piece(k_ref, device, slot, row, 2 * row),
+            piece(v_ref, device, slot, row, 2 * row + 1),
             piece(q_ref, device, slot, 1 - row, 6),
         )
 
@@ -139,13 +139,11 @@
 
         @pl.when(has_rim)
         def _():
-            for base in (0, v_at):
-                pltpu.make_async_remote_copy(
-                    src_ref=buf.at[frame, pl.ds(pl.multiple_of(base + rim_row, cols), cols)],
-                    dst_ref=buf.at[frame, pl.ds(base + two, cols)],
-                    send_sem=rim_send.at[slot], recv_sem=rim_recv.at[slot],
-                    device_id=(rim_frame, rim_pair), device_id_type=MESH,
-                ).start()
+            pltpu.make_async_remote_copy(
+                src_ref=buf.at[frame, pl.ds(rim_row, two)], dst_ref=buf.at[frame, pl.ds(2 * two, two)],
+                send_sem=rim_send.at[slot], recv_sem=rim_recv.at[slot],
+                device_id=(rim_frame, rim_pair), device_id_type=MESH,
+            ).start()
 
     def pass_rims(step, slot):
         for c in range(2):
@@ -154,8 +152,7 @@
     def clear_rim(slot):
         @pl.loop(0, frames)
         def _(frame):
-            for base in (0, v_at):
-                bufs[slot][frame, pl.ds(base + two, cols), :] = jnp.zeros((cols, HEAD_DIM), jnp.bfloat16)
+            bufs[slot][frame, pl.ds(2 * two, two), :] = jnp.zeros((two, HEAD_DIM), jnp.bfloat16)
 
     def wait_rest(slot):
         settle(bufs[slot].at[:, pl.ds(0, keys)], far_recv.at[slot])
@@ -183,13 +180,16 @@
             found.append(jnp.where(spans[j] >= 0, spread, -1))
         return targets, found
 
+    def seen(buf, frame, which):
+        return jnp.concatenate([buf[frame, pl.ds((2 * i + which) * cols, cols), :] for i in range(3)], axis=0)
+
     def attend(group, slot):
         buf = bufs[slot]
         masks = [spreads(frame) for frame in group]
         scores = [
             [
                 lax.dot_general(
-                    buf[frame, pl.ds(q_at, cols), :], buf[target, pl.ds(0, keys), :],
+                    buf[frame, pl.ds(q_at, cols), :], seen(buf, target, 0),
                     (((1,), (1,)), ((), ())), preferred_element_type=jnp.float32,
                 )
                 for target in targets
@@ -206,7 +206,7 @@
         mixed = [
             functools.reduce(jnp.add, [
                 lax.dot_general(
-                    w.astype(jnp.bfloat16), buf[target, pl.ds(v_at, keys), :],
+                    w.astype(jnp.bfloat16), seen(buf, target, 1),
                     (((1,), (0,)), ((), ())), preferred_element_type=jnp.float32,
                 )
                 for w, target in zip(row, targets)

time: 45.7 us -> 45.7 us (level)
  no operation moved by 1% of the time
where the time goes in v6:
time: 45.7 us; the launch traced here: 45.6 us
  Pallas kernels  44.1 us (96%)
  local copies, waits for them, and re-layouts  1.48 us (3%)
    pallas_call x1, Pallas kernels, local(): pl.pallas_call(functools.partial(body, frames, pairs, cols, slots), out_s...  44.1 us
    unnamed x7, local copies, waits for them, and re-layouts  1.48 us

profile of v6, /device:TPU:25, one launch (start us, length us, event | category | flops | bytes accessed | tf_op | source)
XLA Modules:
  0.0 45.6 jit_solution(11064505662154660167)
XLA Ops:
  0.0 0.0 copy-start.1
  0.0 0.0 copy-start
  0.0 0.0 copy-start.2
  0.0 0.7 %copy-done.1 = s32[16,4]{0,1:T(4,128)S(1)} copy-done((s32[16,4]{0,1:T(4,128)S(1)}, s32[16,4]{0,1:T(4,128)}, u32[]{:S(2)}) %copy-start.1) | copy-done | bytes 280
  0.7 0.0 copy-done
  0.7 0.0 copy-done.2
  0.7 44.1 %shard_map.64 = bf16[160,1536]{1,0:T(8,128)(2,1)S(1)} custom-call(s32[4,16]{1,0:T(4,128)S(1)} %bitcast.7, s32[4,16]{1,0:T(4,128)S(1)} %bitcast.8, s32[16]{0:T(128)S(1)} %copy-done.2, bf16[160,1536]{1,0:T(8,128)(2,1)} %bitcast.9, bf16[160,1536]{1,0:T(8,128)(2,1)} %bitcast.10, bf16[160,1536]{1,0:T(8,128)(2,1)} %bitcast.11), custom_call_target="tpu_custom_call" | custom-call | flops 2000000000 | bytes 10000000 | tf_op jit(solution)/shard_map/pallas_call | solution.py:319
  44.8 0.8 %copy.8 = bf16[1,2,80,1536]{3,2,1,0:T(8,128)(2,1)} copy(bf16[1,2,80,1536]{3,2,1,0:T(8,128)(2,1)S(1)} %bitcast.6) | data formatting | bytes 983040
Async XLA Ops:
  0.0 0.7 %copy-start.1 = (s32[16,4]{0,1:T(4,128)S(1)}, s32[16,4]{0,1:T(4,128)}, u32[]{:S(2)}) copy-start(s32[16,4]{0,1:T(4,128)} %param.10) | copy-start | bytes 772
  0.0 0.7 %copy-start = (s32[16,4]{0,1:T(4,128)S(1)}, s32[16,4]{0,1:T(4,128)}, u32[]{:S(2)}) copy-start(s32[16,4]{0,1:T(4,128)} %param.9) | copy-start | bytes 772
  0.0 0.7 %copy-start.2 = (s32[16]{0:T(128)S(1)}, s32[16]{0:T(128)}, u32[]{:S(2)}) copy-start(s32[16]{0:T(128)} %used_hbm.1) | copy-start | bytes 196

commit v7 on v6

--- a/solution.py
+++ b/solution.py
@@ -11,6 +11,7 @@
 HEAD_DIM = 128
 MESH = pl.DeviceIdType.MESH
 NEG = -1e30
+LARGE_CORE = 1
 GROUPS = (8, 4)
 
 
@@ -33,7 +34,7 @@
     rim_row = pl.multiple_of(half * two, two)
 
     def head_of(device, slot):
-        return 3 * (device // 4) + (2 * lax.rem(device, 2) if slot == 0 else 1)
+        return 3 * (device // 4) + (2 * lax.rem(device + LARGE_CORE, 2) if slot == 0 else 1)
 
     def chip(step, sign):
         k = step // 2
@@ -98,7 +99,7 @@
 
     keep(0)
 
-    @pl.when(core == 0)
+    @pl.when(core == LARGE_CORE)
     def _():
         keep(1)
 
@@ -114,7 +115,7 @@
 
     def send_near(step, slot):
         for c in range(2 - slot):
-            device = chip(step, 1) + c
+            device = chip(step, 1) + (c + LARGE_CORE) % 2
 
             @pl.when(device != me)
             def _():
@@ -122,7 +123,7 @@
 
     def send_far(step, slot):
         for c in range(2 - slot):
-            device = chip(step, 1) + c
+            device = chip(step, 1) + (c + LARGE_CORE) % 2
 
             @pl.when(device != me)
             def _():
@@ -255,7 +256,7 @@
     def _(step):
         send_far(step, 1)
 
-        @pl.when(core == 0)
+        @pl.when(core == LARGE_CORE)
         def _():
             pass_rims(step, 1)
 
@@ -273,7 +274,7 @@
         for frame in group_of(step, 2):
             send_out(frame, 0)
 
-    @pl.when(core == 0)
+    @pl.when(core == LARGE_CORE)
     def _():
         wait_rest(1)
 
@@ -291,7 +292,7 @@
     def _():
         settle(buf_a.at[:, pl.ds(0, two)], rim_send.at[0])
 
-    @pl.when(core == 0)
+    @pl.when(core == LARGE_CORE)
     def _():
         settle(buf_b.at[pl.ds(0, frames // 2 - 1), pl.ds(0, 2 * two + cols)], main_send.at[1])
         settle(out_b.at[pl.ds(0, frames - 1)], out_send.at[1])
@@ -300,7 +301,7 @@
         def _():
             settle(buf_b.at[:, pl.ds(0, two)], rim_send.at[1])
 
-    @pl.when(core == 1)
+    @pl.when(core != LARGE_CORE)
     def _():
         settle(buf_b.at[pl.ds(0, frames // 2), pl.ds(0, 2 * two + cols)], main_send.at[1])
 

time: 45.7 us -> 45.4 us (level)
  no operation moved by 1% of the time
where the time goes in v7:
time: 45.4 us; the launch traced here: 45.3 us
  Pallas kernels  43.8 us (96%)
  local copies, waits for them, and re-layouts  1.48 us (3%)
    pallas_call x1, Pallas kernels, local(): pl.pallas_call(functools.partial(body, frames, pairs, cols, slots), out_s...  43.8 us
    unnamed x7, local copies, waits for them, and re-layouts  1.48 us

profile of v7, /device:TPU:25, one launch (start us, length us, event | category | flops | bytes accessed | tf_op | source)
XLA Modules:
  0.0 45.3 jit_solution(15840852030764040229)
XLA Ops:
  0.0 0.0 copy-start.1
  0.0 0.0 copy-start
  0.0 0.0 copy-start.2
  0.0 0.7 %copy-done.1 = s32[16,4]{0,1:T(4,128)S(1)} copy-done((s32[16,4]{0,1:T(4,128)S(1)}, s32[16,4]{0,1:T(4,128)}, u32[]{:S(2)}) %copy-start.1) | copy-done | bytes 280
  0.7 0.0 copy-done
  0.7 0.0 copy-done.2
  0.7 43.8 %shard_map.64 = bf16[160,1536]{1,0:T(8,128)(2,1)S(1)} custom-call(s32[4,16]{1,0:T(4,128)S(1)} %bitcast.7, s32[4,16]{1,0:T(4,128)S(1)} %bitcast.8, s32[16]{0:T(128)S(1)} %copy-done.2, bf16[160,1536]{1,0:T(8,128)(2,1)} %bitcast.9, bf16[160,1536]{1,0:T(8,128)(2,1)} %bitcast.10, bf16[160,1536]{1,0:T(8,128)(2,1)} %bitcast.11), custom_call_target="tpu_custom_call" | custom-call | flops 2000000000 | bytes 10000000 | tf_op jit(solution)/shard_map/pallas_call | solution.py:320
  44.5 0.8 %copy.8 = bf16[1,2,80,1536]{3,2,1,0:T(8,128)(2,1)} copy(bf16[1,2,80,1536]{3,2,1,0:T(8,128)(2,1)S(1)} %bitcast.6) | data formatting | bytes 983040
Async XLA Ops:
  0.0 0.7 %copy-start.1 = (s32[16,4]{0,1:T(4,128)S(1)}, s32[16,4]{0,1:T(4,128)}, u32[]{:S(2)}) copy-start(s32[16,4]{0,1:T(4,128)} %param.10) | copy-start | bytes 772
  0.0 0.7 %copy-start = (s32[16,4]{0,1:T(4,128)S(1)}, s32[16,4]{0,1:T(4,128)}, u32[]{:S(2)}) copy-start(s32[16,4]{0,1:T(4,128)} %param.9) | copy-start | bytes 772
  0.0 0.7 %copy-start.2 = (s32[16]{0:T(128)S(1)}, s32[16]{0:T(128)}, u32[]{:S(2)}) copy-start(s32[16]{0:T(128)} %used_hbm.1) | copy-start | bytes 196

commit v8 on v7

--- a/solution.py
+++ b/solution.py
@@ -16,7 +16,7 @@
 
 
 def body(frames, pairs, cols, slots, kf_hbm, reach_hbm, used_hbm, q_ref, k_ref, v_ref, o_ref,
-         buf_a, buf_b, out_a, out_b, near_recv, far_recv, main_send, rim_send, rim_recv, out_send, out_recv, kf_ref, reach_ref, used_ref, mask_sem):
+         buf_a, buf_b, out_a, out_b, near_recv, far_recv, main_send, rim_send, rim_recv, out_send, out_recv, kf_ref, reach_ref, used_ref, mask_sem, ready):
     me = lax.axis_index("frame")
     pair = lax.axis_index("row")
     core = lax.rem(me, 2)
@@ -51,9 +51,18 @@
 
     barrier = pltpu.get_barrier_semaphore()
 
-    @pl.loop(1, frames)
+    across = me + 2 - 4 * half
+
+    def greet(device):
+        pl.semaphore_signal(barrier, inc=1, device_id=(device, pair), device_id_type=MESH)
+
+    @pl.loop(1, frames // 2)
     def _(d):
-        pl.semaphore_signal(barrier, inc=1, device_id=(lax.rem(me + d, frames), pair), device_id_type=MESH)
+        x = lax.rem(me // 4 + d // 2, 4)
+        greet(4 * x + 2 * half + lax.rem(core + d, 2))
+
+    greet(across)
+    greet(across + 1 - 2 * core)
 
     @pl.when(has_rim)
     def _():
@@ -105,11 +114,13 @@
 
     @pl.when(has_rim)
     def _():
-        pl.semaphore_wait(barrier, frames)
+        pl.semaphore_wait(barrier, frames // 2 + 2)
 
     @pl.when(no_rim)
     def _():
-        pl.semaphore_wait(barrier, frames - 1)
+        pl.semaphore_wait(barrier, frames // 2 + 1)
+
+    pl.semaphore_signal(ready, inc=1, device_id=(across, pair), device_id_type=MESH)
 
     steps = frames // 2
 
@@ -129,10 +140,22 @@
             def _():
                 send(far(device, slot), slot, far_recv.at[slot], device)
 
-    for slot in range(2):
-        @pl.loop(0, steps)
-        def _(step):
-            send_near(step, slot)
+    def early(i):
+        return jnp.where(i == 7, 6, jnp.where(i == 6, 7, jnp.where(i == 5, 4, jnp.where(i == 4, 5, jnp.where(i == 3, 2, jnp.where(i == 2, 3, i))))))
+
+    @pl.loop(0, 3)
+    def _(i):
+        send_near(early(i), 0)
+
+    pl.semaphore_wait(ready, 1)
+
+    @pl.loop(3, steps)
+    def _(i):
+        send_near(early(i), 0)
+
+    @pl.loop(0, steps)
+    def _(step):
+        send_near(step, 1)
 
     def pass_rim(frame, slot):
         buf = bufs[slot]
@@ -249,7 +272,7 @@
 
     @pl.loop(0, steps)
     def _(step):
-        pass_rims(step, 0)
+        pass_rims(early(step), 0)
         send_far(step, 0)
 
     @pl.loop(0, steps)
@@ -333,6 +356,7 @@
             pltpu.SMEM((slots, frames), jnp.int32),
             pltpu.SMEM((frames,), jnp.int32),
             pltpu.SemaphoreType.DMA((3,)),
+            pltpu.SemaphoreType.REGULAR,
         ],
         compiler_params=pltpu.CompilerParams(
             collective_id=0, has_side_effects=True, vmem_limit_bytes=53 * 1024 * 1024

time: 45.4 us -> 45.2 us (level)
  no operation moved by 1% of the time
where the time goes in v8:
time: 45.2 us; the launch traced here: 45.1 us
  Pallas kernels  43.6 us (96%)
  local copies, waits for them, and re-layouts  1.48 us (3%)
    pallas_call x1, Pallas kernels, local(): pl.pallas_call(functools.partial(body, frames, pairs, cols, slots), out_s...  43.6 us
    unnamed x7, local copies, waits for them, and re-layouts  1.48 us

profile of v8, /device:TPU:25, one launch (start us, length us, event | category | flops | bytes accessed | tf_op | source)
XLA Modules:
  0.0 45.1 jit_solution(13131472834737532879)
XLA Ops:
  0.0 0.0 copy-start.1
  0.0 0.0 copy-start
  0.0 0.0 copy-start.2
  0.0 0.7 %copy-done.1 = s32[16,4]{0,1:T(4,128)S(1)} copy-done((s32[16,4]{0,1:T(4,128)S(1)}, s32[16,4]{0,1:T(4,128)}, u32[]{:S(2)}) %copy-start.1) | copy-done | bytes 280
  0.7 0.0 copy-done
  0.7 0.0 copy-done.2
  0.7 43.6 %shard_map.64 = bf16[160,1536]{1,0:T(8,128)(2,1)S(1)} custom-call(s32[4,16]{1,0:T(4,128)S(1)} %bitcast.7, s32[4,16]{1,0:T(4,128)S(1)} %bitcast.8, s32[16]{0:T(128)S(1)} %copy-done.2, bf16[160,1536]{1,0:T(8,128)(2,1)} %bitcast.9, bf16[160,1536]{1,0:T(8,128)(2,1)} %bitcast.10, bf16[160,1536]{1,0:T(8,128)(2,1)} %bitcast.11), custom_call_target="tpu_custom_call" | custom-call | flops 2000000000 | bytes 10000000 | tf_op jit(solution)/shard_map/pallas_call | solution.py:343
  44.3 0.8 %copy.8 = bf16[1,2,80,1536]{3,2,1,0:T(8,128)(2,1)} copy(bf16[1,2,80,1536]{3,2,1,0:T(8,128)(2,1)S(1)} %bitcast.6) | data formatting | bytes 983040
Async XLA Ops:
  0.0 0.7 %copy-start.1 = (s32[16,4]{0,1:T(4,128)S(1)}, s32[16,4]{0,1:T(4,128)}, u32[]{:S(2)}) copy-start(s32[16,4]{0,1:T(4,128)} %param.10) | copy-start | bytes 772
  0.0 0.7 %copy-start = (s32[16,4]{0,1:T(4,128)S(1)}, s32[16,4]{0,1:T(4,128)}, u32[]{:S(2)}) copy-start(s32[16,4]{0,1:T(4,128)} %param.9) | copy-start | bytes 772
  0.0 0.7 %copy-start.2 = (s32[16]{0:T(128)S(1)}, s32[16]{0:T(128)}, u32[]{:S(2)}) copy-start(s32[16]{0:T(128)} %used_hbm.1) | copy-start | bytes 196
